TPU v7x, 128 devices: a whole 4x4x4 slice. The times are simulated.
128 devices in a mesh: space: 16 (over y, z), chan: 8 (over x, core).
Axes of the slice: x: 4, y: 4, z: 4, core: 2. Of those that a mesh axis runs over, the one named last changes fastest.
Arguments:
- field: float32 [128, 512, 512], P('chan', 'space'), may hold values from -6 to 6
- gain_one: float32 [128], P('chan'), may hold values from 0.1 to 1.9
- spec_one: float32 [2, 16, 8, 8], P(None, 'chan'), may hold values from -1.5 to 1.5
- spec_two: float32 [2, 16, 8, 8], P(None, 'chan'), may hold values from -2 to 2
- gain_two: float32 [128], replicated, may hold values from 0.1 to 1.9
- mlp_in: float32 [512, 128], replicated, may hold values from -0.5 to 0.5
- mlp_out: float32 [128, 512], replicated, may hold values from -0.25 to 0.25
Outputs:
- result: float32 [128, 512, 512], P('chan', 'space')
All inputs are finite; a program needn't handle non-finite values.
Results may differ from a plain program's by a relative error of at most 0.00011.
Values sent between devices are 32-bit elements; how exact they have to be, the bound alone decides.
A program may use at most 128 MiB of HBM per device.

v0:
```python
import jax
import jax.numpy as jnp
from jax import lax
from jax.sharding import PartitionSpec as P


def tables(length):
    series = jnp.arange(length, dtype=jnp.int32)
    angle = 2.0 * jnp.pi / length * (series[:, None] * series[None, :] % length).astype(jnp.float32)
    scale = 1.0 / jnp.sqrt(jnp.float32(length))
    return (jnp.cos(angle) * scale, jnp.sin(angle) * scale)


def along_rows(planes, sign):
    cosine, sine = tables(planes.shape[2])
    hi = lax.Precision.HIGHEST
    real_cos = jnp.einsum("chw,hk->ckw", planes[0], cosine, precision=hi)
    real_sin = jnp.einsum("chw,hk->ckw", planes[0], sine, precision=hi)
    imag_cos = jnp.einsum("chw,hk->ckw", planes[1], cosine, precision=hi)
    imag_sin = jnp.einsum("chw,hk->ckw", planes[1], sine, precision=hi)
    return jnp.stack([real_cos - sign * imag_sin, imag_cos + sign * real_sin])


def block_product(real_part, imag_part, weights):
    hi = lax.Precision.HIGHEST
    out_real = jnp.einsum("nihw,nio->nohw", real_part, weights[0], precision=hi) - jnp.einsum(
        "nihw,nio->nohw", imag_part, weights[1], precision=hi
    )
    out_imag = jnp.einsum("nihw,nio->nohw", imag_part, weights[0], precision=hi) + jnp.einsum(
        "nihw,nio->nohw", real_part, weights[1], precision=hi
    )
    return (out_real, out_imag)


def shrink(values):
    return jnp.maximum(values - 0.01, 0.0) + jnp.minimum(values + 0.01, 0.0)


def spectral_mlp(planes, spec_one, spec_two):
    blocks = spec_one.shape[1]
    shape = planes.shape
    width = shape[1] // blocks
    real_part = planes[0].reshape(blocks, width, shape[2], shape[3])
    imag_part = planes[1].reshape(blocks, width, shape[2], shape[3])
    first_real, first_imag = block_product(real_part, imag_part, spec_one)
    second_real, second_imag = block_product(
        jnp.maximum(first_real, 0.0), jnp.maximum(first_imag, 0.0), spec_two
    )
    return jnp.stack(
        [shrink(second_real).reshape(shape[1:]), shrink(second_imag).reshape(shape[1:])]
    )


def local(field, gain_one, spec_one, spec_two, gain_two, mlp_in, mlp_out):
    hi = lax.Precision.HIGHEST
    channels = field.shape[0] * lax.axis_size("chan")
    local_sum = jnp.sum(field, axis=0)
    mean_one = lax.psum(local_sum, "chan") / channels
    centred = field - mean_one
    var_one = lax.psum(jnp.sum(centred * centred, axis=0), "chan") / channels
    normed = (field - mean_one) * lax.rsqrt(var_one + 1e-05) * gain_one[:, None, None]
    col_cos, col_sin = tables(field.shape[2])
    planes = jnp.stack(
        [
            jnp.einsum("chw,wk->chk", normed, col_cos, precision=hi),
            -jnp.einsum("chw,wk->chk", normed, col_sin, precision=hi),
        ]
    )
    columns = lax.all_to_all(planes, "space", split_axis=3, concat_axis=2, tiled=True)
    columns = along_rows(spectral_mlp(along_rows(columns, -1.0), spec_one, spec_two), 1.0)
    planes = lax.all_to_all(columns, "space", split_axis=2, concat_axis=3, tiled=True)
    back = jnp.einsum("chk,kw->chw", planes[0], col_cos, precision=hi) - jnp.einsum(
        "chk,kw->chw", planes[1], col_sin, precision=hi
    )
    mixed = field + back
    cells = lax.all_to_all(mixed, "chan", split_axis=2, concat_axis=0, tiled=True)
    mean_two = jnp.mean(cells, axis=0)
    var_two = jnp.mean((cells - mean_two) ** 2, axis=0)
    normed_two = (cells - mean_two) * lax.rsqrt(var_two + 1e-05) * gain_two[:, None, None]
    hidden = jax.nn.gelu(
        jnp.einsum("dc,chw->dhw", mlp_in, normed_two, precision=hi), approximate=False
    )
    output = cells + jnp.einsum("cd,dhw->chw", mlp_out, hidden, precision=hi)
    return lax.all_to_all(output, "chan", split_axis=0, concat_axis=2, tiled=True)


def solution(mesh):
    placed = (
        P("chan", "space", None),
        P("chan"),
        P(None, "chan", None, None),
        P(None, "chan", None, None),
        P(),
        P(),
        P(),
    )
    return jax.shard_map(
        local, mesh=mesh, in_specs=placed, out_specs=P("chan", "space", None), check_vma=False
    )
```

profile of v0, /device:TPU:1, one launch (start us, length us, event | category | flops | bytes accessed | tf_op | source)
XLA Modules:
  0.0 489.0 jit_solution(288339529328187412)
XLA Ops:
  8.6 60.8 %all-reduce.3.cloned.1.call-done = f32[32,512]{1,0:T(8,128)} async-done(((f32[32,512]{1,0:T(8,128)}), f32[32,512]{1,0:T(8,128)}) %all-reduce.3.cloned.1.call-update) | async-done | bytes 65552 | tf_op jit(solution)/shard_map/psum | solution.py:58
  72.3 57.8 %all-reduce.5.cloned.1.call-done = f32[32,512]{1,0:T(8,128)} async-done(((f32[32,512]{1,0:T(8,128)}), f32[32,512]{1,0:T(8,128)}) %all-reduce.5.cloned.1.call-update) | async-done | bytes 65552 | tf_op jit(solution)/shard_map/psum | solution.py:60
  130.9 7.0 %fusion.108 = f32[1,16,32,512]{3,2,1,0:T(8,128)S(1)} fusion(f32[16,32,512]{2,1,0:T(8,128)} %param.7, f32[16]{0:T(128)} %param.8, f32[32,512]{1,0:T(8,128)S(1)} %add_rsqrt_fusion, f32[32,512]{1,0:T(8,128)S(1)} %broadcast_multiply_fusion), kind=kOutput, calls=%fused_computation.121 | convolution fusion | flops 1615593472 | bytes 2228288 | tf_op jit(solution)/shard_map/chw,wk->chk/dot_general | solution.py:66
  138.0 6.2 %convolution_bitcast_fusion = f32[1,16,32,512]{3,2,1,0:T(8,128)S(1)} fusion(f32[16,32,512]{2,1,0:T(8,128)S(1)} %copy-done.1, f32[16]{0:T(128)S(1)} %copy-done.8, f32[32,512]{1,0:T(8,128)S(1)} %add_rsqrt_fusion, f32[32,512]{1,0:T(8,128)S(1)} %broadcast_multiply_fusion), kind=kOutput, calls=%fused_computation.122 | convolution fusion | flops 1615331328 | bytes 2228288 | tf_op jit(solution)/shard_map/chw,wk->chk/dot_general | solution.py:65
  144.5 7.6 %copy.71 = f32[2,16,32,512]{2,1,0,3:T(8,128)} copy(f32[2,16,32,512]{3,2,1,0:T(8,128)S(1)} %pad_maximum_fusion) | data formatting | bytes 4194304 | tf_op jit(solution)/shard_map/stack | solution.py:63
  152.1 7.4 %reshape.48 = f32[16,1,32768]{2,1,0:T(1,128)S(1)} reshape(f32[512,2,16,32]{3,2,1,0:T(8,128)} %bitcast.290) | data formatting | bytes 4194304
  159.6 30.8 %all_to_all.66 = f32[16,1,32768]{2,1,0:T(1,128)} all-to-all(f32[16,1,32768]{2,1,0:T(1,128)S(1)} %reshape.48), channel_id=1, replica_groups=mesh['space'=16,'chan'=8] {'space'}, dimensions={0} | all-to-all | bytes 4194304 | tf_op jit(solution)/shard_map/all_to_all | solution.py:69
  190.8 7.2 %reduce.2 = f32[16,32768]{1,0:T(8,128)S(1)} reduce(f32[16,1,32768]{2,1,0:T(1,128)} %all_to_all.66, f32[]{:T(128)} %broadcast.182), dimensions={1}, to_apply=%all_to_all.48.reduce_sub_computation | reduce | bytes 4194308 | tf_op jit(solution)/shard_map/all_to_all | solution.py:69
  198.1 4.9 %reshape.49 = f32[512,2,16,32]{3,2,1,0:T(8,128)} reshape(f32[16,32768]{1,0:T(8,128)S(1)} %reduce.2) | data formatting | bytes 4194304
  203.0 8.2 %copy.132 = f32[2,16,32,16,32]{2,3,4,1,0:T(8,128)S(1)} copy(f32[2,16,32,16,32]{2,1,0,4,3:T(8,128)} %bitcast.292) | data formatting | bytes 4194304 | tf_op jit(solution)/shard_map/all_to_all | solution.py:69
  219.5 6.4 %fusion.141 = f32[512,512]{0,1:S(1)} fusion(f32[512,512]{0,1:T(8,128)S(1)} %bitcast.306), kind=kOutput, calls=%fused_computation.163 | convolution fusion | flops 1614544896 | bytes 2097152
  225.9 7.8 %fusion.138 = f32[512,512]{0,1:S(1)} fusion(f32[512,512]{0,1:T(8,128)} %bitcast.307), kind=kOutput, calls=%fused_computation.160 | convolution fusion | flops 1614544896 | bytes 2097152
  233.7 4.4 squeeze.31
  238.1 7.7 %fusion.137 = f32[512,512]{0,1:S(1)} fusion(f32[512,512]{0,1:T(8,128)} %bitcast.308), kind=kOutput, calls=%fused_computation.159 | convolution fusion | flops 1614544896 | bytes 2097152
  245.8 6.8 %fusion.142 = f32[512,512]{0,1:S(1)} fusion(f32[512,512]{0,1:T(8,128)S(1)} %bitcast.309), kind=kOutput, calls=%fused_computation.164 | convolution fusion | flops 1614544896 | bytes 2097152
  264.1 6.6 %fusion.139 = f32[512,512]{0,1:S(1)} fusion(f32[512,512]{0,1:T(8,128)S(1)} %bitcast.311), kind=kOutput, calls=%fused_computation.161 | convolution fusion | flops 1614544896 | bytes 2097152
  270.7 6.4 %fusion.136 = f32[512,512]{0,1:S(1)} fusion(f32[512,512]{0,1:T(8,128)S(1)} %bitcast.312), kind=kOutput, calls=%fused_computation.158 | convolution fusion | flops 1614544896 | bytes 2097152
  278.9 6.4 %fusion.135 = f32[512,512]{0,1:S(1)} fusion(f32[512,512]{0,1:T(8,128)S(1)} %bitcast.313), kind=kOutput, calls=%fused_computation.157 | convolution fusion | flops 1614544896 | bytes 2097152
  285.3 6.6 %fusion.140 = f32[512,512]{0,1:S(1)} fusion(f32[512,512]{0,1:T(8,128)S(1)} %bitcast.314), kind=kOutput, calls=%fused_computation.162 | convolution fusion | flops 1614544896 | bytes 2097152
  292.7 7.6 %copy.87 = f32[2,16,512,32]{3,1,0,2:T(8,128)} copy(f32[2,16,512,32]{2,3,1,0:T(8,128)S(1)} %pad_maximum_fusion.1) | data formatting | bytes 4194304 | tf_op jit(solution)/shard_map/stack | solution.py:21
  300.3 7.4 %reshape.50 = f32[16,1,32768]{2,1,0:T(1,128)S(1)} reshape(f32[512,2,16,32]{3,2,1,0:T(8,128)} %bitcast.291) | data formatting | bytes 4194304
  307.8 27.3 %all_to_all.67 = f32[16,1,32768]{2,1,0:T(1,128)} all-to-all(f32[16,1,32768]{2,1,0:T(1,128)S(1)} %reshape.50), channel_id=1, replica_groups=mesh['space'=16,'chan'=8] {'space'}, dimensions={0} | all-to-all | bytes 4194304 | tf_op jit(solution)/shard_map/all_to_all | solution.py:71
  335.1 7.2 %reduce.3 = f32[16,32768]{1,0:T(8,128)S(1)} reduce(f32[16,1,32768]{2,1,0:T(1,128)} %all_to_all.67, f32[]{:T(128)} %broadcast.182), dimensions={1}, to_apply=%all_to_all.51.reduce_sub_computation | reduce | bytes 4194308 | tf_op jit(solution)/shard_map/all_to_all | solution.py:71
  342.3 5.1 %reshape.51 = f32[512,2,16,32]{3,2,1,0:T(8,128)} reshape(f32[16,32768]{1,0:T(8,128)S(1)} %reduce.3) | data formatting | bytes 4194304
  347.4 8.2 %copy.131 = f32[2,16,16,32,32]{4,2,3,1,0:T(8,128)S(1)} copy(f32[2,16,16,32,32]{4,1,0,3,2:T(8,128)} %bitcast.293) | data formatting | bytes 4194304 | tf_op jit(solution)/shard_map/all_to_all | solution.py:71
  366.5 6.3 %fusion.117 = f32[16,32,512]{2,1,0:T(8,128)S(1)} fusion(f32[16,32,512]{2,1,0:T(8,128)S(1)} %squeeze.36), kind=kOutput, calls=%fused_computation.129 | convolution fusion | flops 1614544896 | bytes 2097152 | tf_op jit(solution)/shard_map/chk,kw->chw/dot_general | solution.py:72
  372.9 6.6 %fusion.103 = f32[16,32,512]{2,1,0:T(8,128)S(1)} fusion(f32[16,32,512]{2,1,0:T(8,128)S(1)} %copy-done.1, f32[16,32,512]{2,1,0:T(8,128)S(1)} %fusion.117, f32[16,32,512]{2,1,0:T(8,128)S(1)} %squeeze.37), kind=kOutput, calls=%fused_computation.111 | convolution fusion | flops 1615069184 | bytes 4194304 | tf_op jit(solution)/shard_map/chk,kw->chw/dot_general | solution.py:72
  383.1 3.9 reshape.52
  387.1 28.7 %all_to_all.68 = f32[8,1,32768]{2,1,0:T(1,128)S(1)} all-to-all(f32[8,1,32768]{2,1,0:T(1,128)S(1)} %reshape.52), channel_id=1, replica_groups=mesh['space'=16,'chan'=8] {'chan'}, dimensions={0} | all-to-all | bytes 2097152 | tf_op jit(solution)/shard_map/all_to_all | solution.py:76
  427.6 7.8 %fusion.68 = f32[32,64,512]{2,1,0:T(8,128)S(1)} fusion(f32[128,32,64]{2,1,0:T(8,128)S(1)} %multiply_multiply_fusion, f32[512,128]{1,0:T(8,128)S(1)} %copy-done), kind=kOutput, calls=%fused_computation.73 | convolution fusion | flops 1610612736 | bytes 5505024 | tf_op jit(solution)/shard_map/dc,chw->dhw/dot_general | solution.py:81
  435.3 13.9 %fusion.109 = f32[128,32,64]{0,2,1:T(8,128)} fusion(f32[128,32,64]{0,2,1:T(8,128)S(1)} %copy.92, f32[32,64,512]{2,1,0:T(8,128)S(1)} %fusion.68, f32[128,512]{1,0:T(8,128)S(1)} %copy-done.7), kind=kOutput, calls=%fused_computation.123 | convolution fusion | flops 1677983744 | bytes 6553600 | tf_op jit(solution)/shard_map/cd,dhw->chw/dot_general | solution.py:83
  453.7 18.5 %all_to_all.69 = f32[8,1,32768]{2,1,0:T(1,128)S(1)} all-to-all(f32[8,1,32768]{2,1,0:T(1,128)S(1)} %reshape.54), channel_id=1, replica_groups=mesh['space'=16,'chan'=8] {'chan'}, dimensions={0} | all-to-all | bytes 2097152 | tf_op jit(solution)/shard_map/all_to_all | solution.py:84
  (63 shorter events, 69.1 us)
Async XLA Ops:
  6.5 421.0 %copy-start = (f32[512,128]{1,0:T(8,128)S(1)}, f32[512,128]{1,0:T(8,128)}, u32[]{:S(2)}) copy-start(f32[512,128]{1,0:T(8,128)} %param.12) | copy-start | bytes 786436
  6.5 131.4 %copy-start.1 = (f32[16,32,512]{2,1,0:T(8,128)S(1)}, f32[16,32,512]{2,1,0:T(8,128)}, u32[]{:S(2)}) copy-start(f32[16,32,512]{2,1,0:T(8,128)} %param.7) | copy-start | bytes 3145732
  6.5 131.5 %copy-start.8 = (f32[16]{0:T(128)S(1)}, f32[16]{0:T(128)}, u32[]{:S(2)}) copy-start(f32[16]{0:T(128)} %param.8) | copy-start | bytes 196
  6.5 62.9 %all-reduce.3.cloned.1.call-start = ((), (), s32[]{:S(2)}) async-start(), calls=%async_computation.4 | async-start | bytes 131072 | tf_op jit(solution)/shard_map/psum | solution.py:58
  8.6 121.5 %all-reduce.5.cloned.1.call-start = ((), (), s32[]{:S(2)}) async-start(), calls=%async_computation.5 | async-start | bytes 131072 | tf_op jit(solution)/shard_map/psum | solution.py:60
  218.5 1.0 copy-start.2
  238.1 7.7 %copy-start.3 = (f32[16,512,32]{1,2,0:T(8,128)S(1)}, f32[16,512,32]{1,2,0:T(8,128)}, u32[]{:S(2)}) copy-start(f32[16,512,32]{1,2,0:T(8,128)} %squeeze.31) | copy-start | bytes 3145732
  252.6 0.7 copy-start.4
  255.0 5.1 %copy-start.5 = (f32[2,2,8,8]{3,2,1,0:T(8,128)S(1)}, f32[2,2,8,8]{3,2,1,0:T(8,128)}, u32[]{:S(2)}) copy-start(f32[2,2,8,8]{3,2,1,0:T(8,128)} %param.10) | copy-start | bytes 3076
  425.4 1.9 copy-start.6
  427.6 7.8 %copy-start.7 = (f32[128,512]{1,0:T(8,128)S(1)}, f32[128,512]{1,0:T(8,128)}, u32[]{:S(2)}) copy-start(f32[128,512]{1,0:T(8,128)} %param.13) | copy-start | bytes 786436
Sparse Core Ops, SparseCore 0:
  9.7 59.7 all-reduce.2
  72.4 57.6 all-reduce.4
where the time goes:
time: 499 us; the launch traced here: 489 us
  waiting for transfers between devices  119 us (24%)
  matrix products  114 us (23%)
  local copies, waits for them, and re-layouts  108 us (22%)
  blocking collectives  105 us (21%)
  other arithmetic  28.6 us (6%)
  between operations  14.3 us (3%)
    psum x1, waiting for transfers between devices, local(): mean_one = lax.psum(local_sum, 'chan') / channels  60.8 us
    psum x1, waiting for transfers between devices, local(): var_one = lax.psum(jnp.sum(centred * centred, axis=0), 'chan') / channels  57.8 us
    unnamed x8, matrix products  54.6 us
    unnamed x26, local copies, waits for them, and re-layouts  35.5 us
    all_to_all x1, blocking collectives, local(): lax.all_to_all(planes, 'space', split_axis=3, concat_axis=2, tiled=True)  30.8 us
    all_to_all x1, blocking collectives, local(): lax.all_to_all(mixed, 'chan', split_axis=2, concat_axis=0, tiled=True)  28.7 us
    all_to_all x1, blocking collectives, local(): lax.all_to_all(columns, 'space', split_axis=2, concat_axis=3, tiled=True)  27.3 us
    all_to_all x1, blocking collectives, local(): lax.all_to_all(output, 'chan', split_axis=0, concat_axis=2, tiled=True)  18.5 us
  transfers between devices with their start and end apart: 2, of which 2 were waited for; matrix products, arithmetic and copies ran while one was open for 0% of the time, Pallas kernels for 0%

commit v1 on v0

v1 whole, which is shorter than its diff:
```python
import functools

import jax
import jax.numpy as jnp
import ml_dtypes
import numpy as np
from jax import lax
from jax.experimental import pallas as pl
from jax.experimental.pallas import tpu as pltpu
from jax.sharding import PartitionSpec as P

MESH = pl.DeviceIdType.MESH
F32 = jnp.float32
BF16 = jnp.bfloat16

H = 512
C = 128
HID = 512
NS = 16
NC = 8
CL = C // NC
HL = H // NS
BS = 8
NBL = CL // BS
KC = 16
ROWS = BS * 2 * KC
LANES = BS * HL

NN = ((1,), (0,))
NT = ((1,), (1,))


def halves(table):
    high = table.astype(ml_dtypes.bfloat16)
    low = (table - high.astype(np.float64)).astype(ml_dtypes.bfloat16)
    return np.stack([high, low])


def width_table():
    row = np.arange(H)
    freq = (row // 32) * KC + row % KC
    imag = (row // KC) % 2 == 1
    nyquist = imag & (freq == 0)
    freq = np.where(nyquist, H // 2, freq)
    angle = 2 * np.pi / H * (freq[:, None] * np.arange(H)[None, :] % H)
    table = np.where((imag & ~nyquist)[:, None], -np.sin(angle), np.cos(angle)) / np.sqrt(H)
    return halves(table)


def height_table():
    series = np.arange(H)
    angle = 2 * np.pi / H * (series[:, None] * series[None, :] % H)
    return halves(np.concatenate([np.cos(angle), np.sin(angle)], axis=1) / np.sqrt(H))


def block_signs():
    row = np.arange(2 * ROWS)[:, None]
    col = np.arange(ROWS)[None, :]
    variant, part_out, part_in = row // ROWS, row // KC % 2, col // KC % 2
    same = row % KC == col % KC
    real = np.where(part_out == part_in, np.where((variant == 1) & (part_out == 1), -1.0, 1.0), 0.0)
    imag = np.where(part_out != part_in, np.where((variant == 0) & (part_out == 0), -1.0, 1.0), 0.0)
    return np.stack([real * same, imag * same]).astype(np.float32)


def channel_lift():
    row = np.arange(2 * ROWS)
    return (row[:, None] // (2 * KC) % BS == np.arange(BS)[None, :]).astype(np.float32)


def split(x):
    high = x.astype(BF16)
    return high, (x - high.astype(F32)).astype(BF16)


def dot(a, b, dims=NN):
    return lax.dot_general(a, b, (dims, ((), ())), preferred_element_type=F32)


def dot3(a, b, dims=NN):
    return dot(a[0], b[0], dims) + (dot(a[0], b[1], dims) + dot(a[1], b[0], dims))


def exact_dot(a, b, dims=NN):
    return lax.dot_general(a, b, (dims, ((), ())), precision=lax.Precision.HIGHEST, preferred_element_type=F32)


def shrink(v):
    return jnp.maximum(v - 0.01, 0.0) + jnp.minimum(v + 0.01, 0.0)


def swap_quarters(t):
    lane = lax.broadcasted_iota(jnp.int32, t[0].shape, 1)
    low = lane < 64
    even = lane % 64 < 32
    u0 = jnp.where(low, t[0], pltpu.roll(t[2], 64, 1))
    u2 = jnp.where(low, pltpu.roll(t[0], 64, 1), t[2])
    u1 = jnp.where(low, t[1], pltpu.roll(t[3], 64, 1))
    u3 = jnp.where(low, pltpu.roll(t[1], 64, 1), t[3])
    v0 = jnp.where(even, u0, pltpu.roll(u1, 32, 1))
    v1 = jnp.where(even, pltpu.roll(u0, 96, 1), u1)
    v2 = jnp.where(even, u2, pltpu.roll(u3, 32, 1))
    v3 = jnp.where(even, pltpu.roll(u2, 96, 1), u3)
    return v0, v1, v2, v3


def kernel(
    gain_one, spec_one, spec_two, gain_two, field, mlp_in, mlp_out, width, height, signs, lift, out,
    f, wd, ht, sg, lf, w1f, w2f, w1h, w1l, w2h, w2l, m1h, m1l, m2h, m2l, x1h, x1l, x2h, x2l,
    part, parts, moments, nh, nl, fwd, got, xh, xl, zh, zl, inv, back, mixed, cells, n2, ob, ps,
    load_sem, send_sem, recv_sem,
):
    me_s = lax.axis_index("space")
    me_c = lax.axis_index("chan")

    barrier = pltpu.get_barrier_semaphore()

    def greet(axis, me, size):
        def one(i, carry):
            pl.semaphore_signal(barrier, inc=1, device_id={axis: lax.rem(me + i, size)}, device_id_type=MESH)
            return carry

        lax.fori_loop(1, size, one, 0)

    greet("chan", me_c, NC)
    greet("space", me_s, NS)

    def cell_block(p):
        return pl.multiple_of(p // 4 * 16, 16), pl.multiple_of(lax.rem(p, 4) * 128, 128)

    def await_bytes(ref, sem):
        pltpu.make_async_copy(ref, ref, sem).wait()

    def send(src, dst, channel, axis, to):
        pltpu.make_async_remote_copy(
            src_ref=src,
            dst_ref=dst,
            send_sem=send_sem.at[channel],
            recv_sem=recv_sem.at[channel],
            device_id={axis: to},
            device_id_type=MESH,
        ).start()

    loads = [(field, f), (signs, sg), (lift, lf), (width, wd), (height, ht), (mlp_in, w1f), (mlp_out, w2f)]
    loads = [pltpu.make_async_copy(src, dst, load_sem.at[i]) for i, (src, dst) in enumerate(loads)]
    for load in loads:
        load.start()
    load_field, load_signs, load_lift, load_width, load_height, load_in, load_out = loads

    load_field.wait()

    def local_moments(p, carry):
        r, c = cell_block(p)
        x = f[:, pl.ds(r, 16), pl.ds(c, 128)]
        total = jnp.sum(x, axis=0)
        d = x - total * (1.0 / CL)
        part[p, 0] = total
        part[p, 1] = jnp.sum(d * d, axis=0)
        return carry

    lax.fori_loop(0, NC, local_moments, 0)
    pl.semaphore_wait(barrier, NC + NS - 2)

    def send_part(i, carry):
        p = lax.rem(me_c + i, NC)
        send(part.at[p], parts.at[me_c], 0, "chan", p)
        return carry

    lax.fori_loop(1, NC, send_part, 0)
    parts[me_c] = part[me_c]

    load_signs.wait()
    load_lift.wait()
    pick = (
        lax.broadcasted_iota(jnp.int32, (4 * BS, 2 * ROWS), 1)
        == KC * lax.broadcasted_iota(jnp.int32, (4 * BS, 2 * ROWS), 0)
    ).astype(BF16)
    spread = (
        lax.broadcasted_iota(jnp.int32, (BS, ROWS), 1) // (2 * KC)
        == lax.broadcasted_iota(jnp.int32, (BS, ROWS), 0)
    ).astype(F32)
    for b in range(NBL):
        real = exact_dot(exact_dot(lf[...], spec_one[0, b], NT), spread)
        imag = exact_dot(exact_dot(lf[...], spec_one[1, b], NT), spread)
        high, low = split(sg[0] * real + sg[1] * imag)
        m1h[b], m1l[b] = high, low
        x1h[b], x1l[b] = dot(pick, high).astype(BF16), dot(pick, low).astype(BF16)
        real = exact_dot(exact_dot(lf[:ROWS], spec_two[0, b], NT), spread)
        imag = exact_dot(exact_dot(lf[:ROWS], spec_two[1, b], NT), spread)
        high, low = split(sg[0, :ROWS] * real + sg[1, :ROWS] * imag)
        m2h[b], m2l[b] = high, low
        pick_two = pick[: 2 * BS, :ROWS]
        x2h[b], x2l[b] = dot(high, pick_two, NT).astype(BF16), dot(low, pick_two, NT).astype(BF16)

    await_bytes(parts.at[pl.ds(0, NC - 1)], recv_sem.at[0])
    totals = parts[:, 0]
    mean = jnp.sum(totals, axis=0) * (1.0 / C)
    apart = totals * (1.0 / CL) - mean
    var = (jnp.sum(parts[:, 1], axis=0) + CL * jnp.sum(apart * apart, axis=0)) * (1.0 / C)
    moments[me_c, 0] = mean
    moments[me_c, 1] = lax.rsqrt(var + 1e-05)

    def send_moments(i, carry):
        send(moments.at[me_c], moments.at[me_c], 1, "chan", lax.rem(me_c + i, NC))
        return carry

    lax.fori_loop(1, NC, send_moments, 0)

    load_in.wait()
    load_out.wait()
    w1h[...], w1l[...] = split(w1f[...] * gain_two[...])
    w2h[...], w2l[...] = split(w2f[...])
    load_width.wait()
    load_height.wait()
    await_bytes(moments.at[pl.ds(0, NC - 1)], recv_sem.at[1])

    for b in range(NBL):

        def normalise(p, carry):
            r, c = cell_block(p)
            mean, scale = moments[p, 0], moments[p, 1]
            for ch in range(BS):
                x = f[BS * b + ch, pl.ds(r, 16), pl.ds(c, 128)]
                high, low = split((x - mean) * scale * gain_one[BS * b + ch])
                row = pl.multiple_of(HL * ch + r, 16)
                nh[pl.ds(row, 16), pl.ds(c, 128)] = high
                nl[pl.ds(row, 16), pl.ds(c, 128)] = low
            return carry

        lax.fori_loop(0, NC, normalise, 0)

        def forward(j, carry):
            k = pl.multiple_of(j * 256, 256)
            table = wd[0, pl.ds(k, 256), :], wd[1, pl.ds(k, 256), :]
            y = dot3(table, (nh[...], nl[...]), NT)
            fwd[b, pl.ds(j * 8, 8)] = y.reshape(8, 2 * KC, LANES)
            return carry

        lax.fori_loop(0, 2, forward, 0)

        def send_slab(i, carry):
            p = lax.rem(me_s + i, NS)
            send(fwd.at[b, p], got.at[b, me_s], 2 + b, "space", p)
            return carry

        lax.fori_loop(1, NS, send_slab, 0)
        got[b, me_s] = fwd[b, me_s]

    column = lax.broadcasted_iota(jnp.int32, (1, KC, 256), 1)
    special = (column == 0) & (me_s == 0)
    keep = jnp.where(special, 0.0, 1.0)
    for b in range(NBL):
        await_bytes(got.at[b, pl.ds(0, NS - 1)], recv_sem.at[2 + b])

        for j in range(4):
            for g in range(2):
                tiles = swap_quarters([got[b, 4 * j + a, :, 128 * g : 128 * g + 128] for a in range(4)])
                for q in range(4):
                    high, low = split(tiles[q])
                    row = (4 * g + q) * 2 * KC
                    xh[row : row + 2 * KC, 128 * j : 128 * j + 128] = high
                    xl[row : row + 2 * KC, 128 * j : 128 * j + 128] = low

        def middle(n, carry):
            lanes = pl.ds(pl.multiple_of(256 * n, 256), 256)
            lanes_two = pl.ds(pl.multiple_of(256 * n + H, 256), 256)
            x = xh[...], xl[...]
            xc = dot3(x, (ht[0, :, lanes], ht[1, :, lanes])).reshape(BS, 2, KC, 256)
            xs = dot3(x, (ht[0, :, lanes_two], ht[1, :, lanes_two])).reshape(BS, 2, KC, 256)
            y = jnp.stack([xc[:, 0] + keep * xs[:, 1], keep * xc[:, 1] - xs[:, 0]], axis=1).reshape(ROWS, 256)
            extra = jnp.stack([xc[:, 1], -xs[:, 1]], axis=1).reshape(ROWS, 256)
            first = jnp.maximum(dot3((m1h[b], m1l[b]), split(y)), 0.0)
            m2 = m2h[b], m2l[b]
            one = shrink(dot3(m2, split(first[:ROWS]))).reshape(BS, 2, KC, 256)
            two = shrink(dot3(m2, split(first[ROWS:]))).reshape(BS, 2, KC, 256)
            real = one[:, 0] + two[:, 0]
            imag = one[:, 1] - two[:, 1]
            first = jnp.maximum(dot3((x1h[b], x1l[b]), split(extra)), 0.0)
            x2 = x2h[b], x2l[b]
            one = shrink(dot3(x2, split(first[: 2 * BS]))).reshape(BS, 2, KC, 256)
            two = shrink(dot3(x2, split(first[2 * BS :]))).reshape(BS, 2, KC, 256)
            z_real = jnp.where(special, 0.5 * (real - (one[:, 1] - two[:, 1])), real)
            z_imag = jnp.where(special, 0.5 * (imag + (one[:, 0] + two[:, 0])), imag)
            zh[:, lanes], zl[:, lanes] = split(jnp.stack([z_real, z_imag], axis=1).reshape(ROWS, 256))
            return carry

        lax.fori_loop(0, 2, middle, 0)

        def inverse(n, carry):
            lanes = pl.ds(pl.multiple_of(256 * n, 256), 256)
            lanes_two = pl.ds(pl.multiple_of(256 * n + H, 256), 256)
            z = zh[...], zl[...]
            zc = dot3(z, (ht[0, :, lanes], ht[1, :, lanes])).reshape(BS, 2, KC, 256)
            zs = dot3(z, (ht[0, :, lanes_two], ht[1, :, lanes_two])).reshape(BS, 2, KC, 256)
            o = jnp.stack([zc[:, 0] - zs[:, 1], zc[:, 1] + zs[:, 0]], axis=1).reshape(ROWS, 256)
            for j in range(2):
                for g in range(2):
                    tiles = swap_quarters(
                        [
                            o[(4 * g + q) * 2 * KC : (4 * g + q + 1) * 2 * KC, 128 * j : 128 * j + 128]
                            for q in range(4)
                        ]
                    )
                    for a in range(4):
                        inv[b, n * 8 + 4 * j + a, :, 128 * g : 128 * g + 128] = tiles[a]
            return carry

        lax.fori_loop(0, 2, inverse, 0)

        def send_rows(i, carry):
            p = lax.rem(me_s + i, NS)
            send(inv.at[b, p], back.at[b, me_s], 4 + b, "space", p)
            return carry

        lax.fori_loop(1, NS, send_rows, 0)
        back[b, me_s] = inv[b, me_s]

    me_r, me_w = cell_block(me_c)
    for b in range(NBL):
        await_bytes(back.at[b, pl.ds(0, NS - 1)], recv_sem.at[4 + b])
        nh[...], nl[...] = split(back[b].reshape(H, LANES).T)

        def residual(n, carry):
            lanes = pl.ds(pl.multiple_of(256 * n, 256), 256)
            y = dot3((nh[...], nl[...]), (wd[0, :, lanes], wd[1, :, lanes])).reshape(BS, HL, 256)
            mixed[BS * b : BS * b + BS, :, lanes] = f[BS * b : BS * b + BS, :, lanes] + y
            return carry

        lax.fori_loop(0, 2, residual, 0)

        for t in range(2):

            def send_cells(i, carry):
                p = lax.rem(me_c + i, NC)
                r, c = cell_block(p)
                send(
                    mixed.at[pl.ds(BS * b, BS), pl.ds(pl.multiple_of(r + 8 * t, 8), 8), pl.ds(c, 128)],
                    cells.at[me_c, pl.ds(BS * b, BS), pl.ds(8 * t, 8)],
                    6 + 2 * b + t,
                    "chan",
                    p,
                )
                return carry

            lax.fori_loop(1, NC, send_cells, 0)
        cells[me_c, BS * b : BS * b + BS] = mixed[BS * b : BS * b + BS, pl.ds(me_r, 16), pl.ds(me_w, 128)]

    own = []
    for t in range(2):
        for b in range(NBL):
            await_bytes(cells.at[pl.ds(0, NC - 1), pl.ds(BS * b, BS), pl.ds(8 * t, 8)], recv_sem.at[6 + 2 * b + t])
        x = cells[:, :, 8 * t : 8 * t + 8].reshape(C, 8, 128)
        mean = jnp.sum(x, axis=0) * (1.0 / C)
        d = x - mean
        scale = lax.rsqrt(jnp.sum(d * d, axis=0) * (1.0 / C) + 1e-05)
        n2[...] = (d * scale).reshape(C * 8, 128)

        def channel_mlp(j, carry):
            x = jnp.concatenate([n2[pl.ds(2 * j + i, C, stride=8), :] for i in range(2)], axis=1)
            v = dot3((w1h[...], w1l[...]), split(x))
            v = 0.5 * v * (1.0 + lax.erf(v * (2.0**-0.5)))
            y = dot3((w2h[...], w2l[...]), split(v))
            for i in range(2):
                ob[pl.ds(2 * j + i, C, stride=8), :] = y[:, 128 * i : 128 * i + 128]
            return carry

        lax.fori_loop(0, 4, channel_mlp, 0)
        ps[t] = cells[:, :, 8 * t : 8 * t + 8] + ob[...].reshape(NC, CL, 8, 128)

        rows = pl.ds(pl.multiple_of(me_r + 8 * t, 8), 8)
        place = out.at[:, rows, pl.ds(me_w, 128)]

        def send_result(i, carry):
            p = lax.rem(me_c + i, NC)
            send(ps.at[t, p], place, 10 + t, "chan", p)
            return carry

        lax.fori_loop(1, NC, send_result, 0)
        own.append(pltpu.make_async_copy(ps.at[t, me_c], place, load_sem.at[7 + t]))
        own[t].start()

    for t in range(2):
        own[t].wait()
        await_bytes(ps.at[t, pl.ds(0, NC - 1)], recv_sem.at[10 + t])

    await_bytes(part.at[pl.ds(0, NC - 1)], send_sem.at[0])
    await_bytes(parts.at[pl.ds(0, NC - 1)], send_sem.at[1])
    for b in range(NBL):
        await_bytes(fwd.at[b, pl.ds(0, NS - 1)], send_sem.at[2 + b])
        await_bytes(inv.at[b, pl.ds(0, NS - 1)], send_sem.at[4 + b])
    for t in range(2):
        for b in range(NBL):
            await_bytes(cells.at[pl.ds(0, NC - 1), pl.ds(BS * b, BS), pl.ds(8 * t, 8)], send_sem.at[6 + 2 * b + t])
        await_bytes(ps.at[t, pl.ds(0, NC - 1)], send_sem.at[10 + t])


def local(field, gain_one, spec_one, spec_two, gain_two, mlp_in, mlp_out):
    vmem = pl.BlockSpec(memory_space=pltpu.VMEM)
    smem = pl.BlockSpec(memory_space=pltpu.SMEM)
    hbm = pl.BlockSpec(memory_space=pl.ANY)
    tables = [jnp.asarray(width_table()), jnp.asarray(height_table())]
    tables += [jnp.asarray(block_signs()), jnp.asarray(channel_lift())]
    scratch = [
        ((CL, HL, H), F32),
        ((2, H, H), BF16),
        ((2, H, 2 * H), BF16),
        ((2, 2 * ROWS, ROWS), F32),
        ((2 * ROWS, BS), F32),
        ((HID, C), F32),
        ((C, HID), F32),
        ((HID, C), BF16),
        ((HID, C), BF16),
        ((C, HID), BF16),
        ((C, HID), BF16),
        ((NBL, 2 * ROWS, ROWS), BF16),
        ((NBL, 2 * ROWS, ROWS), BF16),
        ((NBL, ROWS, ROWS), BF16),
        ((NBL, ROWS, ROWS), BF16),
        ((NBL, 4 * BS, ROWS), BF16),
        ((NBL, 4 * BS, ROWS), BF16),
        ((NBL, ROWS, 2 * BS), BF16),
        ((NBL, ROWS, 2 * BS), BF16),
        ((NC, 2, 16, 128), F32),
        ((NC, 2, 16, 128), F32),
        ((NC, 2, 16, 128), F32),
        ((LANES, H), BF16),
        ((LANES, H), BF16),
        ((NBL, NS, 2 * KC, LANES), F32),
        ((NBL, NS, 2 * KC, LANES), F32),
        ((ROWS, H), BF16),
        ((ROWS, H), BF16),
        ((ROWS, H), BF16),
        ((ROWS, H), BF16),
        ((NBL, NS, 2 * KC, LANES), F32),
        ((NBL, NS, 2 * KC, LANES), F32),
        ((CL, HL, H), F32),
        ((NC, CL, 16, 128), F32),
        ((C * 8, 128), F32),
        ((C * 8, 128), F32),
        ((2, NC, CL, 8, 128), F32),
    ]
    return pl.pallas_call(
        kernel,
        out_shape=jax.ShapeDtypeStruct((CL, HL, H), F32),
        in_specs=[smem, vmem, vmem, vmem] + [hbm] * 7,
        out_specs=hbm,
        scratch_shapes=[pltpu.VMEM(shape, dtype) for shape, dtype in scratch]
        + [pltpu.SemaphoreType.DMA((9,)), pltpu.SemaphoreType.DMA((12,)), pltpu.SemaphoreType.DMA((12,))],
        compiler_params=pltpu.CompilerParams(
            collective_id=0, has_side_effects=True, vmem_limit_bytes=56 * 1024 * 1024
        ),
        name="afno_block",
    )(gain_one, spec_one, spec_two, gain_two.reshape(1, C), field, mlp_in, mlp_out, *tables)


def solution(mesh):
    placed = (
        P("chan", "space", None),
        P("chan"),
        P(None, "chan", None, None),
        P(None, "chan", None, None),
        P(),
        P(),
        P(),
    )
    return jax.shard_map(
        local, mesh=mesh, in_specs=placed, out_specs=P("chan", "space", None), check_vma=False
    )
```

time: 499 us -> 78.4 us (0.16); the launches traced: 489 us -> 78.2 us
  waiting for transfers between devices: 119 us -> 0 us
  matrix products: 114 us -> 0 us
  local copies, waits for them, and re-layouts: 108 us -> 2.29 us
  blocking collectives: 105 us -> 0 us
  Pallas kernels: 0 us -> 75.9 us
  other arithmetic: 28.6 us -> 0 us
  between operations: 14.3 us -> 0.01 us
    psum x2 -> x0, waiting for transfers between devices: 119 us -> none  [the longest x1 60.8 us: local(): mean_one = lax.psum(local_sum, 'chan') / channels]
    all_to_all x4 -> x0, blocking collectives: 105 us -> none  [the longest x1 30.8 us: local(): lax.all_to_all(planes, 'space', split_axis=3, concat_axis=2, tiled=True)]
    pallas_call x0 -> x1, Pallas kernels: none -> 75.9 us  [local(): pl.pallas_call(kernel, out_shape=jax.ShapeDtypeStruct((CL, HL, H), F32),...]
    dot_general x14 -> x0, matrix products: 59.2 us -> none  [the longest x1 13.9 us: local(): output = cells + jnp.einsum('cd,dhw->chw', mlp_out, hidden, precision=hi)]
    unnamed x8 -> x0, matrix products: 54.6 us -> none
    unnamed x26 -> x1, local copies, waits for them, and re-layouts: 35.5 us -> 2.29 us
    all_to_all x7 -> x0, local copies, waits for them, and re-layouts: 27.2 us -> none  [the longest x2 8.72 us: local(): lax.all_to_all(planes, 'space', split_axis=3, concat_axis=2, tiled=True)]
    all_to_all x4 -> x0, other arithmetic: 20.5 us -> none  [the longest x1 7.21 us: local(): lax.all_to_all(columns, 'space', split_axis=2, concat_axis=3, tiled=True)]
  transfers between devices with their start and end apart: 2 -> 0, of which waited for: 2 -> 0; matrix products, arithmetic and copies ran while one was open for 0% -> 0% of each run, Pallas kernels for 0% -> 0%
where the time goes in v1:
time: 78.4 us; the launch traced here: 78.2 us
  Pallas kernels  75.9 us (97%)
  local copies, waits for them, and re-layouts  2.29 us (3%)
    pallas_call x1, Pallas kernels, local(): pl.pallas_call(kernel, out_shape=jax.ShapeDtypeStruct((CL, HL, H), F32),...  75.9 us
    unnamed x1, local copies, waits for them, and re-layouts  2.29 us

profile of v1, /device:TPU:1, one launch (start us, length us, event | category | flops | bytes accessed | tf_op | source)
XLA Modules:
  0.0 78.2 jit_solution(10551507485724709133)
XLA Ops:
  0.0 75.9 %afno_block.1 = f32[16,32,512]{2,1,0:T(8,128)} custom-call(f32[16]{0:T(128)} %gain_one.1, f32[2,2,8,8]{3,2,1,0:T(8,128)} %spec_one.1, f32[2,2,8,8]{3,2,1,0:T(8,128)} %spec_two.1, f32[1,128]{1,0:T(1,128)} %bitcast.1, f32[16,32,512]{2,1,0:T(8,128)} %field.1, f32[512,128]{1,0:T(8,128)} %mlp_in.1, f32[128,512]{1,0:T(8,128)} %mlp_out.1, ...), custom_call_target="tpu_custom_call" | custom-call | tf_op jit(solution)/shard_map/afno_block/pallas_call | solution.py:442
  75.9 2.3 %copy.13 = f32[16,32,512]{2,1,0:T(8,128)} copy(f32[16,32,512]{2,1,0:T(8,128)} %afno_block.1) | data formatting | bytes 2097152

commit v2 on v1

v2 whole, which is shorter than its diff:
```python
import functools

import jax
import jax.numpy as jnp
import ml_dtypes
import numpy as np
from jax import lax
from jax.experimental import pallas as pl
from jax.experimental.pallas import tpu as pltpu
from jax.sharding import PartitionSpec as P

MESH = pl.DeviceIdType.MESH
F32 = jnp.float32
BF16 = jnp.bfloat16

H = 512
C = 128
HID = 512
NS = 16
NC = 8
CL = C // NC
HL = H // NS
BS = 8
NBL = CL // BS
KC = 16
ROWS = BS * 2 * KC
LANES = BS * HL
HALF = H // 2

NN = ((1,), (0,))
NT = ((1,), (1,))


def halves(table):
    high = table.astype(ml_dtypes.bfloat16)
    low = (table - high.astype(np.float64)).astype(ml_dtypes.bfloat16)
    return np.stack([high, low])


def width_table():
    row = np.arange(HALF)
    number = (row // (2 * KC)) * KC + row % KC
    imag = (row // KC) % 2 == 1
    both = []
    for odd in (0, 1):
        nyquist = imag & (number == 0) & (odd == 0)
        freq = np.where(nyquist, H // 2, 2 * number + odd)
        angle = 2 * np.pi / H * (freq[:, None] * np.arange(HALF)[None, :] % H)
        both.append(np.where((imag & ~nyquist)[:, None], -np.sin(angle), np.cos(angle)) / np.sqrt(H))
    return halves(np.stack(both))


def height_table():
    series = np.arange(HALF)
    ways = []
    for odd in (0, 1):
        angle = 2 * np.pi / H * (series[:, None] * (2 * series + odd)[None, :] % H)
        ways.append((np.cos(angle), np.sin(angle)))
    there = np.stack([np.concatenate([c, s], axis=1) for c, s in ways])
    back = np.stack([np.concatenate([c.T, s.T], axis=1) for c, s in ways])
    return halves(np.stack([there, back]) / np.sqrt(H))


def split(x):
    high = x.astype(BF16)
    return high, (x - high.astype(F32)).astype(BF16)


def dot(a, b, dims=NN):
    return lax.dot_general(a, b, (dims, ((), ())), preferred_element_type=F32)


def dot3(a, b, dims=NN):
    left = jnp.concatenate([a[0], a[0], a[1]], axis=dims[0][0])
    right = jnp.concatenate([b[0], b[1], b[0]], axis=dims[1][0])
    return dot(left, right, dims)


def exact_dot(a, b, dims=NN):
    return lax.dot_general(a, b, (dims, ((), ())), precision=lax.Precision.HIGHEST, preferred_element_type=F32)


def iota(shape, axis):
    return lax.broadcasted_iota(jnp.int32, shape, axis)


def gelu(v):
    return 0.5 * v * (1.0 + lax.erf(v * 2.0**-0.5))


def shrink(v):
    return jnp.maximum(v - 0.01, 0.0) + jnp.minimum(v + 0.01, 0.0)


def swap_quarters(t):
    lane = lax.broadcasted_iota(jnp.int32, t[0].shape, 1)
    low = lane < 64
    even = lane % 64 < 32
    u0 = jnp.where(low, t[0], pltpu.roll(t[2], 64, 1))
    u2 = jnp.where(low, pltpu.roll(t[0], 64, 1), t[2])
    u1 = jnp.where(low, t[1], pltpu.roll(t[3], 64, 1))
    u3 = jnp.where(low, pltpu.roll(t[1], 64, 1), t[3])
    v0 = jnp.where(even, u0, pltpu.roll(u1, 32, 1))
    v1 = jnp.where(even, pltpu.roll(u0, 96, 1), u1)
    v2 = jnp.where(even, u2, pltpu.roll(u3, 32, 1))
    v3 = jnp.where(even, pltpu.roll(u2, 96, 1), u3)
    return v0, v1, v2, v3


def kernel(
    gain_one, spec_one, spec_two, gain_two, field, mlp_in, mlp_out, width, height, out,
    f, wd, ht, w1f, w2f, w1h, w1l, w2h, w2l, rw, m1h, m1l, m2h, m2l, x1h, x1l, x2h, x2l,
    part, parts, moments, nh, nl, fwd, got, xh, xl, zh, zl, inv, back, mixed, cells, n2, ob, ps,
    load_sem, send_sem, recv_sem,
):
    me_s = lax.axis_index("space")
    me_c = lax.axis_index("chan")

    loads = [(field.at[:, pl.ds(16 * i, 16)], f.at[:, pl.ds(16 * i, 16)]) for i in range(2)]
    loads += [(width, wd), (height, ht), (mlp_in, w1f), (mlp_out, w2f)]
    loads = [pltpu.make_async_copy(src, dst, load_sem.at[i]) for i, (src, dst) in enumerate(loads)]
    for load in loads:
        load.start()
    load_width, load_height, load_in, load_out = loads[2:]

    barrier = pltpu.get_barrier_semaphore()

    def greet(axis, me, size):
        def one(i, carry):
            pl.semaphore_signal(barrier, inc=1, device_id={axis: lax.rem(me + i, size)}, device_id_type=MESH)
            return carry

        lax.fori_loop(1, size, one, 0)

    greet("chan", me_c, NC)
    greet("space", me_s, NS)

    def cell_block(p):
        return pl.multiple_of(p // 4 * 16, 16), pl.multiple_of(lax.rem(p, 4) * 128, 128)

    def arrive(ref, channel):
        pltpu.make_async_copy(ref, ref, recv_sem.at[channel]).wait()

    def leave(ref, channel):
        pltpu.make_async_copy(ref, ref, send_sem.at[channel]).wait()

    def send(src, dst, channel, axis, to):
        pltpu.make_async_remote_copy(
            src_ref=src,
            dst_ref=dst,
            send_sem=send_sem.at[channel],
            recv_sem=recv_sem.at[channel],
            device_id={axis: to},
            device_id_type=MESH,
        ).start()

    def local_moments(p, carry):
        r, c = cell_block(p)
        x = f[:, pl.ds(r, 16), pl.ds(c, 128)]
        total = jnp.sum(x, axis=0)
        d = x - total * (1.0 / CL)
        part[p, 0] = total
        part[p, 1] = jnp.sum(d * d, axis=0)
        return carry

    for i in range(2):
        loads[i].wait()
        lax.fori_loop(4 * i, 4 * i + 4, local_moments, 0)
    pl.semaphore_wait(barrier, NC + NS - 2)

    def send_part(i, carry):
        p = lax.rem(me_c + i, NC)
        send(part.at[p], parts.at[me_c], 0, "chan", p)
        return carry

    lax.fori_loop(1, NC, send_part, 0)
    parts[me_c] = part[me_c]

    lift = jnp.concatenate(
        [
            iota((4 * BS, BS), 0) // 2 % BS == iota((4 * BS, BS), 1),
            iota((4 * BS, BS), 0) % BS == iota((4 * BS, BS), 1),
        ],
        axis=0,
    ).astype(F32)
    weights = jnp.concatenate([spec_one[...].reshape(4 * BS, BS), spec_two[...].reshape(4 * BS, BS)], axis=0)
    lifted = exact_dot(lift, weights, NT)
    high = lifted.astype(BF16)
    rest = lifted - high.astype(F32)
    middle_term = rest.astype(BF16)
    low = (rest - middle_term.astype(F32)).astype(BF16)
    wide = (iota((8 * BS, 8 * ROWS), 1) // (2 * KC) == iota((8 * BS, 8 * ROWS), 0)).astype(BF16)
    lane = iota((8 * BS, 8 * 128), 1)
    slim = ((lane // 128 * BS + lane % BS == iota((8 * BS, 8 * 128), 0)) & (lane % 128 < 2 * BS)).astype(BF16)

    def spread(rows, table):
        terms = jnp.concatenate([high[rows], middle_term[rows], low[rows]], axis=0)
        terms = dot(terms, table)
        return terms[: 4 * BS] + (terms[4 * BS : 8 * BS] + terms[8 * BS :])

    def complex_form(values, width, part_out, part_in, layer, b):
        variant = iota((4 * BS, width), 0) // (2 * BS)
        real = values[:, (4 * layer + b) * width : (4 * layer + b + 1) * width]
        imag = values[:, (4 * layer + 2 + b) * width : (4 * layer + 2 + b + 1) * width]
        real = jnp.where((variant == 1) & (part_out == 1), -real, real)
        imag = jnp.where((variant == 0) & (part_out == 0), -imag, imag)
        return jnp.where(part_out == part_in, real, imag)

    big = spread(slice(0, 4 * BS), wide)
    small = spread(slice(4 * BS, 8 * BS), slim)
    same_column = iota((KC, ROWS), 1) % KC == iota((KC, ROWS), 0)
    for b in range(NBL):
        for layer in range(2):
            part_out, part_in = iota((4 * BS, ROWS), 0) % 2, iota((4 * BS, ROWS), 1) // KC % 2
            rw[2 * b + layer] = complex_form(big, ROWS, part_out, part_in, layer, b)
            for r in range(4 * BS if layer == 0 else 2 * BS):
                row_high, row_low = split(jnp.where(same_column, rw[2 * b + layer, r : r + 1, :], 0.0))
                to_high, to_low = ((m1h, m1l), (m2h, m2l))[layer]
                to_high[b, KC * r : KC * r + KC] = row_high
                to_low[b, KC * r : KC * r + KC] = row_low
            part_out, part_in = iota((4 * BS, 128), 0) // BS % 2, iota((4 * BS, 128), 1) // BS % 2
            form = complex_form(small, 128, part_out, part_in, layer, b)
            if layer == 0:
                x1h[b], x1l[b] = split(form)
            else:
                x2h[b], x2l[b] = split(form[: 2 * BS])

    arrive(parts.at[pl.ds(0, NC - 1)], 0)
    totals = parts[:, 0]
    mean = jnp.sum(totals, axis=0) * (1.0 / C)
    apart = totals * (1.0 / CL) - mean
    var = (jnp.sum(parts[:, 1], axis=0) + CL * jnp.sum(apart * apart, axis=0)) * (1.0 / C)
    moments[me_c, 0] = mean
    moments[me_c, 1] = lax.rsqrt(var + 1e-05)

    def send_moments(i, carry):
        send(moments.at[me_c], moments.at[me_c], 1, "chan", lax.rem(me_c + i, NC))
        return carry

    lax.fori_loop(1, NC, send_moments, 0)

    load_in.wait()
    load_out.wait()
    w1h[...], w1l[...] = split(w1f[...] * gain_two[...])
    w2h[...], w2l[...] = split(w2f[...])
    load_width.wait()
    load_height.wait()
    arrive(moments.at[pl.ds(0, NC - 1)], 1)

    for b in range(NBL):

        for i in range(4):
            p = 4 * (i // 2) + i % 2
            r, c = i // 2 * 16, i % 2 * 128
            mean, scale = moments[p, 0], moments[p, 1]
            mean_two, scale_two = moments[p + 2, 0], moments[p + 2, 1]
            for ch in range(BS):
                x = (f[BS * b + ch, r : r + 16, c : c + 128] - mean) * scale
                x_two = (f[BS * b + ch, r : r + 16, HALF + c : HALF + c + 128] - mean_two) * scale_two
                x, x_two = x * gain_one[BS * b + ch], x_two * gain_one[BS * b + ch]
                rows, lanes = slice(HL * ch + r, HL * ch + r + 16), slice(c, c + 128)
                nh[0, rows, lanes], nl[0, rows, lanes] = split(x + x_two)
                nh[1, rows, lanes], nl[1, rows, lanes] = split(x - x_two)

        for j in range(2):
            y = dot3((wd[0, j], wd[1, j]), (nh[j], nl[j]), NT)
            fwd[b, 8 * j : 8 * j + 8] = y.reshape(8, 2 * KC, LANES)

        def send_slab(i, carry):
            p = lax.rem(me_s + i, NS)
            send(fwd.at[b, p], got.at[b, me_s], 2 + b, "space", p)
            return carry

        lax.fori_loop(1, NS, send_slab, 0)
        got[b, me_s] = fwd[b, me_s]

    special = (iota((KC, H), 0) == 0) & (me_s == 0)
    keep = jnp.where(special, 0.0, 1.0)
    for b in range(NBL):
        arrive(got.at[b, pl.ds(0, NS - 1)], 2 + b)

        for j in range(2):
            for g in range(2):
                lanes = slice(128 * g, 128 * g + 128)
                tiles = swap_quarters([got[b, 4 * j + a, :, lanes] for a in range(4)])
                tiles_two = swap_quarters([got[b, 4 * (j + 2) + a, :, lanes] for a in range(4)])
                for q in range(4):
                    rows = slice((4 * g + q) * 2 * KC, (4 * g + q + 1) * 2 * KC)
                    to = slice(128 * j, 128 * j + 128)
                    xh[0, rows, to], xl[0, rows, to] = split(tiles[q] + tiles_two[q])
                    xh[1, rows, to], xl[1, rows, to] = split(tiles[q] - tiles_two[q])

        both = []
        for n in range(2):
            x = dot3((xh[n], xl[n]), (ht[0, 0, n], ht[1, 0, n]))
            both.append((x[:, :HALF], x[:, HALF:]))
        xc, xs = (jnp.concatenate(pair, axis=1).reshape(BS, 2, KC, H) for pair in zip(*both))
        y = jnp.stack([xc[:, 0] + keep * xs[:, 1], keep * xc[:, 1] - xs[:, 0]], axis=1).reshape(ROWS, H)
        first = jnp.maximum(dot3((m1h[b], m1l[b]), split(y)), 0.0)
        m2 = m2h[b], m2l[b]
        one = shrink(dot3(m2, split(first[:ROWS]))).reshape(BS, 2, KC, H)
        two = shrink(dot3(m2, split(first[ROWS:]))).reshape(BS, 2, KC, H)
        real = one[:, 0] + two[:, 0]
        imag = one[:, 1] - two[:, 1]
        channel = iota((BS, H), 0)
        extra_real, extra_imag = jnp.zeros((BS, H), F32), jnp.zeros((BS, H), F32)
        for ch in range(BS):
            extra_real = jnp.where(channel == ch, xc[ch, 1, 0:1], extra_real)
            extra_imag = jnp.where(channel == ch, -xs[ch, 1, 0:1], extra_imag)
        extra = jnp.concatenate([extra_real, extra_imag], axis=0)
        first = jnp.maximum(dot3((x1h[b, :, : 2 * BS], x1l[b, :, : 2 * BS]), split(extra)), 0.0)
        x2 = x2h[b, :, : 2 * BS], x2l[b, :, : 2 * BS]
        one = shrink(dot3(x2, split(first[: 2 * BS])))
        two = shrink(dot3(x2, split(first[2 * BS :])))
        extra_real = one[:BS] + two[:BS]
        extra_imag = one[BS:] - two[BS:]
        for ch in range(BS):
            z_real = jnp.where(special, 0.5 * (real[ch] - extra_imag[ch : ch + 1]), real[ch])
            z_imag = jnp.where(special, 0.5 * (imag[ch] + extra_real[ch : ch + 1]), imag[ch])
            for i, z in enumerate((z_real, z_imag)):
                rows = slice((2 * ch + i) * KC, (2 * ch + i + 1) * KC)
                for n in range(2):
                    zh[n, rows], zl[n, rows] = split(z[:, HALF * n : HALF * n + HALF])

        halves_of = []
        for n in range(2):
            z = dot3((zh[n], zl[n]), (ht[0, 1, n], ht[1, 1, n]))
            zc = z[:, :HALF].reshape(BS, 2, KC, HALF)
            zs = z[:, HALF:].reshape(BS, 2, KC, HALF)
            halves_of.append(jnp.stack([zc[:, 0] - zs[:, 1], zc[:, 1] + zs[:, 0]], axis=1).reshape(ROWS, HALF))
        halves_of = halves_of[0] + halves_of[1], halves_of[0] - halves_of[1]
        for j in range(4):
            for g in range(2):
                lanes = slice(128 * (j % 2), 128 * (j % 2) + 128)
                rows = [slice((4 * g + q) * 2 * KC, (4 * g + q + 1) * 2 * KC) for q in range(4)]
                tiles = swap_quarters([halves_of[j // 2][rows[q], lanes] for q in range(4)])
                for a in range(4):
                    inv[b, 4 * j + a, :, 128 * g : 128 * g + 128] = tiles[a]

        def send_rows(i, carry):
            p = lax.rem(me_s + i, NS)
            send(inv.at[b, p], back.at[b, me_s], 4 + b, "space", p)
            return carry

        lax.fori_loop(1, NS, send_rows, 0)
        back[b, me_s] = inv[b, me_s]

    me_r, me_w = cell_block(me_c)
    for b in range(NBL):
        arrive(back.at[b, pl.ds(0, NS - 1)], 4 + b)
        channels = slice(BS * b, BS * b + BS)
        sums = []
        for j in range(2):
            columns = split(back[b, 8 * j : 8 * j + 8].reshape(HALF, LANES).T)
            sums.append(dot3(columns, (wd[0, j], wd[1, j])))
        mixed[channels, :, :HALF] = f[channels, :, :HALF] + (sums[0] + sums[1]).reshape(BS, HL, HALF)
        mixed[channels, :, HALF:] = f[channels, :, HALF:] + (sums[0] - sums[1]).reshape(BS, HL, HALF)

        for t in range(2):

            def send_cells(i, carry):
                p = lax.rem(me_c + i, NC)
                r, c = cell_block(p)
                send(
                    mixed.at[pl.ds(BS * b, BS), pl.ds(pl.multiple_of(r + 8 * t, 8), 8), pl.ds(c, 128)],
                    cells.at[me_c, pl.ds(BS * b, BS), pl.ds(8 * t, 8)],
                    6 + 2 * b + t,
                    "chan",
                    p,
                )
                return carry

            lax.fori_loop(1, NC, send_cells, 0)
        cells[me_c, BS * b : BS * b + BS] = mixed[BS * b : BS * b + BS, pl.ds(me_r, 16), pl.ds(me_w, 128)]

    own = []
    for t in range(2):
        for b in range(NBL):
            arrive(cells.at[pl.ds(0, NC - 1), pl.ds(BS * b, BS), pl.ds(8 * t, 8)], 6 + 2 * b + t)
        x = cells[:, :, 8 * t : 8 * t + 8].reshape(C, 8, 128)
        mean = jnp.sum(x, axis=0) * (1.0 / C)
        d = x - mean
        scale = lax.rsqrt(jnp.sum(d * d, axis=0) * (1.0 / C) + 1e-05)
        n2[...] = (d * scale).reshape(C * 8, 128)

        x = jnp.concatenate([n2[pl.ds(i, C, stride=8), :] for i in range(8)], axis=1)
        v = gelu(dot3((w1h[...], w1l[...]), split(x)))
        y = dot3((w2h[...], w2l[...]), split(v))
        for i in range(8):
            ob[pl.ds(i, C, stride=8), :] = y[:, 128 * i : 128 * i + 128]
        ps[t] = cells[:, :, 8 * t : 8 * t + 8] + ob[...].reshape(NC, CL, 8, 128)

        rows = pl.ds(pl.multiple_of(me_r + 8 * t, 8), 8)
        place = out.at[:, rows, pl.ds(me_w, 128)]

        def send_result(i, carry):
            p = lax.rem(me_c + i, NC)
            send(ps.at[t, p], place, 10 + t, "chan", p)
            return carry

        lax.fori_loop(1, NC, send_result, 0)
        own.append(pltpu.make_async_copy(ps.at[t, me_c], place, load_sem.at[6 + t]))
        own[t].start()

    for t in range(2):
        own[t].wait()
        arrive(ps.at[t, pl.ds(0, NC - 1)], 10 + t)

    leave(part.at[pl.ds(0, NC - 1)], 0)
    leave(parts.at[pl.ds(0, NC - 1)], 1)
    for b in range(NBL):
        leave(fwd.at[b, pl.ds(0, NS - 1)], 2 + b)
        leave(inv.at[b, pl.ds(0, NS - 1)], 4 + b)
    for t in range(2):
        for b in range(NBL):
            leave(cells.at[pl.ds(0, NC - 1), pl.ds(BS * b, BS), pl.ds(8 * t, 8)], 6 + 2 * b + t)
        leave(ps.at[t, pl.ds(0, NC - 1)], 10 + t)


def local(field, gain_one, spec_one, spec_two, gain_two, mlp_in, mlp_out):
    vmem = pl.BlockSpec(memory_space=pltpu.VMEM)
    smem = pl.BlockSpec(memory_space=pltpu.SMEM)
    hbm = pl.BlockSpec(memory_space=pl.ANY)
    tables = [jnp.asarray(width_table()), jnp.asarray(height_table())]
    scratch = [
        ((CL, HL, H), F32),
        ((2, 2, HALF, HALF), BF16),
        ((2, 2, 2, HALF, H), BF16),
        ((HID, C), F32),
        ((C, HID), F32),
        ((HID, C), BF16),
        ((HID, C), BF16),
        ((C, HID), BF16),
        ((C, HID), BF16),
        ((2 * NBL, 4 * BS, ROWS), F32),
        ((NBL, 2 * ROWS, ROWS), BF16),
        ((NBL, 2 * ROWS, ROWS), BF16),
        ((NBL, ROWS, ROWS), BF16),
        ((NBL, ROWS, ROWS), BF16),
        ((NBL, 4 * BS, 128), BF16),
        ((NBL, 4 * BS, 128), BF16),
        ((NBL, 2 * BS, 128), BF16),
        ((NBL, 2 * BS, 128), BF16),
        ((NC, 2, 16, 128), F32),
        ((NC, 2, 16, 128), F32),
        ((NC, 2, 16, 128), F32),
        ((2, LANES, HALF), BF16),
        ((2, LANES, HALF), BF16),
        ((NBL, NS, 2 * KC, LANES), F32),
        ((NBL, NS, 2 * KC, LANES), F32),
        ((2, ROWS, HALF), BF16),
        ((2, ROWS, HALF), BF16),
        ((2, ROWS, HALF), BF16),
        ((2, ROWS, HALF), BF16),
        ((NBL, NS, 2 * KC, LANES), F32),
        ((NBL, NS, 2 * KC, LANES), F32),
        ((CL, HL, H), F32),
        ((NC, CL, 16, 128), F32),
        ((C * 8, 128), F32),
        ((C * 8, 128), F32),
        ((2, NC, CL, 8, 128), F32),
    ]
    return pl.pallas_call(
        kernel,
        out_shape=pltpu.VMEM((CL, HL, H), F32),
        in_specs=[smem, vmem, vmem, vmem] + [hbm] * 5,
        out_specs=pl.BlockSpec(memory_space=pltpu.VMEM),
        scratch_shapes=[pltpu.VMEM(shape, dtype) for shape, dtype in scratch]
        + [pltpu.SemaphoreType.DMA((8,)), pltpu.SemaphoreType.DMA((12,)), pltpu.SemaphoreType.DMA((12,))],
        compiler_params=pltpu.CompilerParams(
            collective_id=0, has_side_effects=True, vmem_limit_bytes=56 * 1024 * 1024
        ),
        name="afno_block",
    )(gain_one, spec_one, spec_two, gain_two.reshape(1, C), field, mlp_in, mlp_out, *tables)


def solution(mesh):
    placed = (
        P("chan", "space", None),
        P("chan"),
        P(None, "chan", None, None),
        P(None, "chan", None, None),
        P(),
        P(),
        P(),
    )
    return jax.shard_map(
        local, mesh=mesh, in_specs=placed, out_specs=P("chan", "space", None), check_vma=False
    )
```

time: 78.4 us -> 69.2 us (0.88); the launches traced: 78.2 us -> 68 us
  Pallas kernels: 75.9 us -> 67 us
  local copies, waits for them, and re-layouts: 2.29 us -> 0.97 us
    pallas_call x1, Pallas kernels: 75.9 us -> 67 us  [local(): pl.pallas_call(kernel, out_shape=pltpu.VMEM((CL, HL, H), F32), in_specs=[...]
    unnamed x1, local copies, waits for them, and re-layouts: 2.29 us -> 0.97 us
where the time goes in v2:
time: 69.2 us; the launch traced here: 68 us
  Pallas kernels  67 us (97%)
  local copies, waits for them, and re-layouts  0.97 us (1%)
    pallas_call x1, Pallas kernels, local(): pl.pallas_call(kernel, out_shape=pltpu.VMEM((CL, HL, H), F32), in_specs=[...  67 us

profile of v2, /device:TPU:1, one launch (start us, length us, event | category | flops | bytes accessed | tf_op | source)
XLA Modules:
  0.0 68.0 jit_solution(9490980582939841794)
XLA Ops:
  0.0 67.0 %afno_block.1 = f32[16,32,512]{2,1,0:T(8,128)S(1)} custom-call(f32[16]{0:T(128)} %gain_one.1, f32[2,2,8,8]{3,2,1,0:T(8,128)} %spec_one.1, f32[2,2,8,8]{3,2,1,0:T(8,128)} %spec_two.1, f32[1,128]{1,0:T(1,128)} %bitcast.1, f32[16,32,512]{2,1,0:T(8,128)} %field.1, f32[512,128]{1,0:T(8,128)} %mlp_in.1, f32[128,512]{1,0:T(8,128)} %mlp_out.1, ...), custom_call_target="tpu_custom_call" | custom-call | tf_op jit(solution)/shard_map/afno_block/pallas_call | solution.py:463
  67.0 1.0 %copy.11 = f32[16,32,512]{2,1,0:T(8,128)} copy(f32[16,32,512]{2,1,0:T(8,128)S(1)} %afno_block.1) | data formatting | bytes 2097152

commit v3 on v2

v3 whole, which is shorter than its diff:
```python
import functools

import jax
import jax.numpy as jnp
import ml_dtypes
import numpy as np
from jax import lax
from jax.experimental import pallas as pl
from jax.experimental.pallas import tpu as pltpu
from jax.sharding import PartitionSpec as P

MESH = pl.DeviceIdType.MESH
F32 = jnp.float32
BF16 = jnp.bfloat16

H = 512
C = 128
HID = 512
NS = 16
NC = 8
CL = C // NC
HL = H // NS
BS = 8
NBL = CL // BS
KC = 16
ROWS = BS * 2 * KC
HALF = H // 2
HH = HL // 2

NN = ((1,), (0,))
NT = ((1,), (1,))


def halves(table):
    high = table.astype(ml_dtypes.bfloat16)
    low = (table - high.astype(np.float64)).astype(ml_dtypes.bfloat16)
    return np.stack([high, low])


def width_table():
    row = np.arange(HALF)
    number = (row // (2 * KC)) * KC + row % KC
    imag = (row // KC) % 2 == 1
    both = []
    for odd in (0, 1):
        nyquist = imag & (number == 0) & (odd == 0)
        freq = np.where(nyquist, H // 2, 2 * number + odd)
        angle = 2 * np.pi / H * (freq[:, None] * np.arange(HALF)[None, :] % H)
        both.append(np.where((imag & ~nyquist)[:, None], -np.sin(angle), np.cos(angle)) / np.sqrt(H))
    return halves(np.stack(both))


def height_table():
    index = np.arange(HALF)
    h = index % 128 // HH * HL + index // 128 * HH + index % HH
    there, back = [], []
    for odd in (0, 1):
        angle = 2 * np.pi / H * (h[:, None] * (2 * index + odd)[None, :] % H)
        cosine, sine = np.cos(angle) / np.sqrt(H), np.sin(angle) / np.sqrt(H)
        there.append(np.concatenate([cosine, sine], axis=1))
        back.append(np.stack([np.concatenate([cosine.T[:, k], sine.T[:, k]], axis=1) for k in np.split(index, 2)]))
    return halves(np.stack(there)), halves(np.stack(back))


def split(x):
    high = x.astype(BF16)
    return high, (x - high.astype(F32)).astype(BF16)


def dot(a, b, dims=NN):
    return lax.dot_general(a, b, (dims, ((), ())), preferred_element_type=F32)


def dot3(a, b, dims=NN):
    left = jnp.concatenate([a[0], a[0], a[1]], axis=dims[0][0])
    right = jnp.concatenate([b[0], b[1], b[0]], axis=dims[1][0])
    return dot(left, right, dims)


def exact_dot(a, b, dims=NN):
    return lax.dot_general(a, b, (dims, ((), ())), precision=lax.Precision.HIGHEST, preferred_element_type=F32)


def iota(shape, axis):
    return lax.broadcasted_iota(jnp.int32, shape, axis)


def gelu(v):
    return 0.5 * v * (1.0 + lax.erf(v * 2.0**-0.5))


def shrink(v):
    return jnp.maximum(v - 0.01, 0.0) + jnp.minimum(v + 0.01, 0.0)


def swap_eighths(tiles):
    tiles = list(tiles)
    lane = iota(tiles[0].shape, 1)
    for step in (4, 2, 1):
        width = 16 * step
        low = lane // width % 2 == 0
        for i in range(8):
            if i & step == 0:
                one, two = tiles[i], tiles[i + step]
                tiles[i] = jnp.where(low, one, pltpu.roll(two, width, 1))
                tiles[i + step] = jnp.where(low, pltpu.roll(one, 128 - width, 1), two)
    return tiles


def kernel(
    gain_one, spec_one, spec_two, gain_two, field, mlp_in, mlp_out, width, there, here, out,
    f, wd, ht, hb, w1f, w2f, w1h, w1l, w2h, w2l, rw, m1h, m1l, m2h, m2l, x1h, x1l, x2h, x2l,
    part, parts, moments, nh, nl, fwd, got, xh, xl, zh, zl, inv, back, mixed, cells, n2, ob, ps,
    load_sem, send_sem, recv_sem,
):
    me_s = lax.axis_index("space")
    me_c = lax.axis_index("chan")

    loads = [(field.at[:, pl.ds(16 * i, 16)], f.at[:, pl.ds(16 * i, 16)]) for i in range(2)]
    loads += [(width, wd), (there, ht), (here, hb), (mlp_in, w1f), (mlp_out, w2f)]
    loads = [pltpu.make_async_copy(src, dst, load_sem.at[i]) for i, (src, dst) in enumerate(loads)]
    for load in loads[:2]:
        load.start()
    load_width, load_there, load_here, load_in, load_out = loads[2:]

    barrier = pltpu.get_barrier_semaphore()

    def greet(axis, me, size):
        def one(i, carry):
            pl.semaphore_signal(barrier, inc=1, device_id={axis: lax.rem(me + i, size)}, device_id_type=MESH)
            return carry

        lax.fori_loop(1, size, one, 0)

    greet("chan", me_c, NC)
    greet("space", me_s, NS)

    def cell_block(p, t):
        return (
            pl.ds(pl.multiple_of(t * HH + p // 4 * 8, 8), 8),
            pl.ds(pl.multiple_of(lax.rem(p, 4) * 128, 128), 128),
        )

    flight = {}

    def arrive(ref, channel):
        pltpu.make_async_copy(ref, ref, recv_sem.at[channel]).wait()

    def leave(channel):
        ref = flight.pop(channel)
        pltpu.make_async_copy(ref, ref, send_sem.at[channel]).wait()

    def send_all(channel, axis, pair):
        me, size = (me_c, NC) if axis == "chan" else (me_s, NS)

        def one(i, carry):
            if axis == "chan":
                p = lax.rem(me // 2 + i // 2 + 2, 4) * 2 + lax.rem(me + i, 2)
            else:
                p = lax.rem(me // 4 + i // 4 + 2, 4) * 4 + lax.rem(me + i + 2, 4)
            src, dst = pair(p)
            pltpu.make_async_remote_copy(
                src_ref=src,
                dst_ref=dst,
                send_sem=send_sem.at[channel],
                recv_sem=recv_sem.at[channel],
                device_id={axis: p},
                device_id_type=MESH,
            ).start()
            return carry

        own = 4 if axis == "chan" else 10
        lax.fori_loop(0, own, one, 0)
        lax.fori_loop(own + 1, size, one, 0)

    for t in range(2):
        loads[t].wait()

        for p in range(NC):
            r, c = HH * t + 8 * (p // 4), 128 * (p % 4)
            x = f[:, r : r + 8, c : c + 128]
            total = jnp.sum(x, axis=0)
            d = x - total * (1.0 / CL)
            part[t, p, 0] = total
            part[t, p, 1] = jnp.sum(d * d, axis=0)
    for load in loads[2:]:
        load.start()
    pl.semaphore_wait(barrier, NC + NS - 2)
    for t in range(2):
        send_all(t, "chan", lambda p: (part.at[t, p], parts.at[t, me_c]))
        flight[t] = part.at[t, pl.ds(0, NC - 1)]
        parts[t, me_c] = part[t, me_c]

    lift = jnp.concatenate(
        [
            iota((4 * BS, BS), 0) // 2 % BS == iota((4 * BS, BS), 1),
            iota((4 * BS, BS), 0) % BS == iota((4 * BS, BS), 1),
        ],
        axis=0,
    ).astype(F32)
    weights = jnp.concatenate([spec_one[...].reshape(4 * BS, BS), spec_two[...].reshape(4 * BS, BS)], axis=0)
    lifted = exact_dot(lift, weights, NT)
    high = lifted.astype(BF16)
    rest = lifted - high.astype(F32)
    middle_term = rest.astype(BF16)
    low = (rest - middle_term.astype(F32)).astype(BF16)
    wide = (iota((8 * BS, 8 * ROWS), 1) // (2 * KC) == iota((8 * BS, 8 * ROWS), 0)).astype(BF16)
    lane = iota((8 * BS, 8 * 128), 1)
    slim = ((lane // 128 * BS + lane % BS == iota((8 * BS, 8 * 128), 0)) & (lane % 128 < 2 * BS)).astype(BF16)

    def spread(rows, table):
        terms = jnp.concatenate([high[rows], middle_term[rows], low[rows]], axis=0)
        terms = dot(terms, table)
        return terms[: 4 * BS] + (terms[4 * BS : 8 * BS] + terms[8 * BS :])

    def complex_form(values, width, part_out, part_in, layer, b):
        variant = iota((4 * BS, width), 0) // (2 * BS)
        real = values[:, (4 * layer + b) * width : (4 * layer + b + 1) * width]
        imag = values[:, (4 * layer + 2 + b) * width : (4 * layer + 2 + b + 1) * width]
        real = jnp.where((variant == 1) & (part_out == 1), -real, real)
        imag = jnp.where((variant == 0) & (part_out == 0), -imag, imag)
        return jnp.where(part_out == part_in, real, imag)

    big = spread(slice(0, 4 * BS), wide)
    small = spread(slice(4 * BS, 8 * BS), slim)
    same_column = iota((KC, ROWS), 1) % KC == iota((KC, ROWS), 0)
    for b in range(NBL):
        for layer in range(2):
            part_out, part_in = iota((4 * BS, ROWS), 0) % 2, iota((4 * BS, ROWS), 1) // KC % 2
            rw[2 * b + layer] = complex_form(big, ROWS, part_out, part_in, layer, b)
            for r in range(4 * BS if layer == 0 else 2 * BS):
                row_high, row_low = split(jnp.where(same_column, rw[2 * b + layer, r : r + 1, :], 0.0))
                to_high, to_low = ((m1h, m1l), (m2h, m2l))[layer]
                to_high[b, KC * r : KC * r + KC] = row_high
                to_low[b, KC * r : KC * r + KC] = row_low
            part_out, part_in = iota((4 * BS, 128), 0) // BS % 2, iota((4 * BS, 128), 1) // BS % 2
            form = complex_form(small, 128, part_out, part_in, layer, b)
            if layer == 0:
                x1h[b], x1l[b] = split(form)
            else:
                x2h[b], x2l[b] = split(form[: 2 * BS])

    for t in range(2):
        arrive(parts.at[t, pl.ds(0, NC - 1)], t)
        totals = parts[t, :, 0]
        mean = jnp.sum(totals, axis=0) * (1.0 / C)
        apart = totals * (1.0 / CL) - mean
        var = (jnp.sum(parts[t, :, 1], axis=0) + CL * jnp.sum(apart * apart, axis=0)) * (1.0 / C)
        moments[t, me_c, 0] = mean
        moments[t, me_c, 1] = lax.rsqrt(var + 1e-05)

        send_all(2 + t, "chan", lambda p: (moments.at[t, me_c], moments.at[t, me_c]))
        flight[2 + t] = moments.at[t, pl.ds(0, NC - 1)]

    load_in.wait()
    load_out.wait()
    w1h[...], w1l[...] = split(w1f[...] * gain_two[...])
    w2h[...], w2l[...] = split(w2f[...])
    load_width.wait()

    def send_slab(t, b):
        channel = 4 + 2 * t + b
        send_all(channel, "space", lambda p: (fwd.at[t, b, p], got.at[t, b, me_s]))
        flight[channel] = fwd.at[t, b, pl.ds(0, NS - 1)]
        got[t, b, me_s] = fwd[t, b, me_s]

    for t in range(2):
        arrive(moments.at[t, pl.ds(0, NC - 1)], 2 + t)
        for i in range(2):
            both = []
            for k in (i, i + 2):
                both.append([jnp.concatenate([moments[t, k, m], moments[t, k + 4, m]], axis=0) for m in range(2)])
            for ch in range(CL):
                x, x_two = (
                    (f[ch, HH * t : HH * t + HH, c : c + 128] - mean) * scale * gain_one[ch]
                    for c, (mean, scale) in zip((128 * i, HALF + 128 * i), both)
                )
                rows, lanes = slice(HH * ch, HH * ch + HH), slice(128 * i, 128 * i + 128)
                nh[0, rows, lanes], nl[0, rows, lanes] = split(x + x_two)
                nh[1, rows, lanes], nl[1, rows, lanes] = split(x - x_two)

        for j in range(2):
            y = dot3((wd[0, j], wd[1, j]), (nh[j], nl[j]), NT)
            for b in range(NBL):
                fwd[t, b, 8 * j : 8 * j + 8] = y[:, 128 * b : 128 * b + 128].reshape(8, 2 * KC, 128)

        send_slab(t, 0)
    leave(4)
    leave(6)
    send_slab(0, 1)
    send_slab(1, 1)
    load_there.wait()
    load_here.wait()

    special = (iota((KC, H), 0) == 0) & (me_s == 0)
    keep = jnp.where(special, 0.0, 1.0)

    def send_rows(b, t):
        channel = 8 + 2 * b + t
        send_all(channel, "space", lambda p: (inv.at[b, t, p], back.at[b, t, me_s]))
        flight[channel] = inv.at[b, t, pl.ds(0, NS - 1)]
        back[b, t, me_s] = inv[b, t, me_s]

    def spectral(b, between=None):
        for t in range(2):
            arrive(got.at[t, b, pl.ds(0, NS - 1)], 4 + 2 * t + b)

        for t in range(2):
            near = swap_eighths([got[t, b, a] for a in range(8)])
            far = swap_eighths([got[t, b, 8 + a] for a in range(8)])
            for ch in range(BS):
                rows, lanes = slice(2 * KC * ch, 2 * KC * ch + 2 * KC), slice(128 * t, 128 * t + 128)
                xh[0, rows, lanes], xl[0, rows, lanes] = split(near[ch] + far[ch])
                xh[1, rows, lanes], xl[1, rows, lanes] = split(near[ch] - far[ch])

        both = []
        for n in range(2):
            x = dot3((xh[n], xl[n]), (ht[0, n], ht[1, n]))
            both.append((x[:, :HALF], x[:, HALF:]))
        xc, xs = (jnp.concatenate(pair, axis=1).reshape(BS, 2, KC, H) for pair in zip(*both))
        y = jnp.stack([xc[:, 0] + keep * xs[:, 1], keep * xc[:, 1] - xs[:, 0]], axis=1).reshape(ROWS, H)
        first = jnp.maximum(dot3((m1h[b], m1l[b]), split(y)), 0.0)
        m2 = m2h[b], m2l[b]
        one = shrink(dot3(m2, split(first[:ROWS]))).reshape(BS, 2, KC, H)
        two = shrink(dot3(m2, split(first[ROWS:]))).reshape(BS, 2, KC, H)
        real = one[:, 0] + two[:, 0]
        imag = one[:, 1] - two[:, 1]
        channel = iota((BS, H), 0)
        extra_real, extra_imag = jnp.zeros((BS, H), F32), jnp.zeros((BS, H), F32)
        for ch in range(BS):
            extra_real = jnp.where(channel == ch, xc[ch, 1, 0:1], extra_real)
            extra_imag = jnp.where(channel == ch, -xs[ch, 1, 0:1], extra_imag)
        extra = jnp.concatenate([extra_real, extra_imag], axis=0)
        first = jnp.maximum(dot3((x1h[b, :, : 2 * BS], x1l[b, :, : 2 * BS]), split(extra)), 0.0)
        x2 = x2h[b, :, : 2 * BS], x2l[b, :, : 2 * BS]
        one = shrink(dot3(x2, split(first[: 2 * BS])))
        two = shrink(dot3(x2, split(first[2 * BS :])))
        extra_real = one[:BS] + two[:BS]
        extra_imag = one[BS:] - two[BS:]
        for ch in range(BS):
            z_real = jnp.where(special, 0.5 * (real[ch] - extra_imag[ch : ch + 1]), real[ch])
            z_imag = jnp.where(special, 0.5 * (imag[ch] + extra_real[ch : ch + 1]), imag[ch])
            for i, z in enumerate((z_real, z_imag)):
                rows = slice((2 * ch + i) * KC, (2 * ch + i + 1) * KC)
                for n in range(2):
                    zh[n, rows], zl[n, rows] = split(z[:, HALF * n : HALF * n + HALF])

        if between is not None:
            between()
        for t in range(2):
            sums = []
            for n in range(2):
                z = dot3((zh[n], zl[n]), (hb[0, n, t], hb[1, n, t]))
                zc = z[:, :128].reshape(BS, 2, KC, 128)
                zs = z[:, 128:].reshape(BS, 2, KC, 128)
                sums.append(jnp.stack([zc[:, 0] - zs[:, 1], zc[:, 1] + zs[:, 0]], axis=1).reshape(BS, 2 * KC, 128))
            near = swap_eighths([sums[0][ch] + sums[1][ch] for ch in range(BS)])
            far = swap_eighths([sums[0][ch] - sums[1][ch] for ch in range(BS)])
            for a in range(8):
                inv[b, t, a] = near[a]
                inv[b, t, 8 + a] = far[a]
            if t == 0:
                send_rows(b, t)

    def residual(b, t):
        channels = slice(BS * b, BS * b + BS)
        arrive(back.at[b, t, pl.ds(0, NS - 1)], 8 + 2 * b + t)
        sums = []
        for j in range(2):
            columns = split(back[b, t, 8 * j : 8 * j + 8].reshape(HALF, 128).T)
            sums.append(dot3(columns, (wd[0, j], wd[1, j])))
        rows = slice(HH * t, HH * t + HH)
        mixed[channels, rows, :HALF] = f[channels, rows, :HALF] + (sums[0] + sums[1]).reshape(BS, HH, HALF)
        mixed[channels, rows, HALF:] = f[channels, rows, HALF:] + (sums[0] - sums[1]).reshape(BS, HH, HALF)

        def pair(p):
            rows, lanes = cell_block(p, t)
            return mixed.at[pl.ds(BS * b, BS), rows, lanes], cells.at[t, me_c, pl.ds(BS * b, BS)]

        channel = 12 + 2 * b + t
        send_all(channel, "chan", pair)
        flight[channel] = cells.at[t, pl.ds(0, NC - 1), pl.ds(BS * b, BS)]
        rows, lanes = cell_block(me_c, t)
        cells[t, me_c, channels] = mixed[channels, rows, lanes]

    own = []

    def channel_mlp(t):
        for b in range(NBL):
            arrive(cells.at[t, pl.ds(0, NC - 1), pl.ds(BS * b, BS)], 12 + 2 * b + t)
        x = cells[t].reshape(C, 8, 128)
        mean = jnp.sum(x, axis=0) * (1.0 / C)
        d = x - mean
        scale = lax.rsqrt(jnp.sum(d * d, axis=0) * (1.0 / C) + 1e-05)
        n2[...] = (d * scale).reshape(C * 8, 128)
        x = jnp.concatenate([n2[pl.ds(i, C, stride=8), :] for i in range(8)], axis=1)
        v = gelu(dot3((w1h[...], w1l[...]), split(x)))
        y = dot3((w2h[...], w2l[...]), split(v))
        for i in range(8):
            ob[pl.ds(i, C, stride=8), :] = y[:, 128 * i : 128 * i + 128]
        ps[t] = cells[t] + ob[...].reshape(NC, CL, 8, 128)

        rows, lanes = cell_block(me_c, t)
        place = out.at[:, rows, lanes]
        send_all(16 + t, "chan", lambda p: (ps.at[t, p], place))
        flight[16 + t] = ps.at[t, pl.ds(0, NC - 1)]
        own.append(pltpu.make_async_copy(ps.at[t, me_c], place, load_sem.at[7 + t]))
        own[t].start()

    spectral(0)
    leave(8)
    send_rows(0, 1)
    spectral(1, lambda: residual(0, 0))
    residual(0, 1)
    leave(10)
    send_rows(1, 1)
    residual(1, 0)
    residual(1, 1)
    for t in range(2):
        channel_mlp(t)
    for t in range(2):
        own[t].wait()
        arrive(ps.at[t, pl.ds(0, NC - 1)], 16 + t)
    for channel in sorted(flight):
        leave(channel)


def local(field, gain_one, spec_one, spec_two, gain_two, mlp_in, mlp_out):
    vmem = pl.BlockSpec(memory_space=pltpu.VMEM)
    smem = pl.BlockSpec(memory_space=pltpu.SMEM)
    hbm = pl.BlockSpec(memory_space=pl.ANY)
    tables = [jnp.asarray(table) for table in (width_table(), *height_table())]
    scratch = [
        ((CL, HL, H), F32),
        ((2, 2, HALF, HALF), BF16),
        ((2, 2, HALF, H), BF16),
        ((2, 2, 2, HALF, HALF), BF16),
        ((HID, C), F32),
        ((C, HID), F32),
        ((HID, C), BF16),
        ((HID, C), BF16),
        ((C, HID), BF16),
        ((C, HID), BF16),
        ((2 * NBL, 4 * BS, ROWS), F32),
        ((NBL, 2 * ROWS, ROWS), BF16),
        ((NBL, 2 * ROWS, ROWS), BF16),
        ((NBL, ROWS, ROWS), BF16),
        ((NBL, ROWS, ROWS), BF16),
        ((NBL, 4 * BS, 128), BF16),
        ((NBL, 4 * BS, 128), BF16),
        ((NBL, 2 * BS, 128), BF16),
        ((NBL, 2 * BS, 128), BF16),
        ((2, NC, 2, 8, 128), F32),
        ((2, NC, 2, 8, 128), F32),
        ((2, NC, 2, 8, 128), F32),
        ((2, CL * HH, HALF), BF16),
        ((2, CL * HH, HALF), BF16),
        ((2, 2, NS, 2 * KC, 128), F32),
        ((2, 2, NS, 2 * KC, 128), F32),
        ((2, ROWS, HALF), BF16),
        ((2, ROWS, HALF), BF16),
        ((2, ROWS, HALF), BF16),
        ((2, ROWS, HALF), BF16),
        ((2, 2, NS, 2 * KC, 128), F32),
        ((2, 2, NS, 2 * KC, 128), F32),
        ((CL, HL, H), F32),
        ((2, NC, CL, 8, 128), F32),
        ((C * 8, 128), F32),
        ((C * 8, 128), F32),
        ((2, NC, CL, 8, 128), F32),
    ]
    return pl.pallas_call(
        kernel,
        out_shape=pltpu.VMEM((CL, HL, H), F32),
        in_specs=[smem, vmem, vmem, vmem] + [hbm] * 6,
        out_specs=pl.BlockSpec(memory_space=pltpu.VMEM),
        scratch_shapes=[pltpu.VMEM(shape, dtype) for shape, dtype in scratch]
        + [pltpu.SemaphoreType.DMA((9,)), pltpu.SemaphoreType.DMA((18,)), pltpu.SemaphoreType.DMA((18,))],
        compiler_params=pltpu.CompilerParams(
            collective_id=0, has_side_effects=True, vmem_limit_bytes=56 * 1024 * 1024
        ),
        name="afno_block",
    )(gain_one, spec_one, spec_two, gain_two.reshape(1, C), field, mlp_in, mlp_out, *tables)


def solution(mesh):
    placed = (
        P("chan", "space", None),
        P("chan"),
        P(None, "chan", None, None),
        P(None, "chan", None, None),
        P(),
        P(),
        P(),
    )
    return jax.shard_map(
        local, mesh=mesh, in_specs=placed, out_specs=P("chan", "space", None), check_vma=False
    )
```

time: 69.2 us -> 65.3 us (0.944); the launches traced: 68 us -> 65.1 us
  Pallas kernels: 67 us -> 64.1 us
    pallas_call x1, Pallas kernels: 67 us -> 64.1 us  [local(): pl.pallas_call(kernel, out_shape=pltpu.VMEM((CL, HL, H), F32), in_specs=[...]
where the time goes in v3:
time: 65.3 us; the launch traced here: 65.1 us
  Pallas kernels  64.1 us (98%)
  local copies, waits for them, and re-layouts  0.97 us (1%)
    pallas_call x1, Pallas kernels, local(): pl.pallas_call(kernel, out_shape=pltpu.VMEM((CL, HL, H), F32), in_specs=[...  64.1 us

profile of v3, /device:TPU:1, one launch (start us, length us, event | category | flops | bytes accessed | tf_op | source)
XLA Modules:
  0.0 65.1 jit_solution(12974025709096835863)
XLA Ops:
  0.0 64.1 %afno_block.1 = f32[16,32,512]{2,1,0:T(8,128)S(1)} custom-call(f32[16]{0:T(128)} %gain_one.1, f32[2,2,8,8]{3,2,1,0:T(8,128)} %spec_one.1, f32[2,2,8,8]{3,2,1,0:T(8,128)} %spec_two.1, f32[1,128]{1,0:T(1,128)} %bitcast.1, f32[16,32,512]{2,1,0:T(8,128)} %field.1, f32[512,128]{1,0:T(8,128)} %mlp_in.1, f32[128,512]{1,0:T(8,128)} %mlp_out.1, ...), custom_call_target="tpu_custom_call" | custom-call | tf_op jit(solution)/shard_map/afno_block/pallas_call | solution.py:472
  64.1 1.0 %copy.12 = f32[16,32,512]{2,1,0:T(8,128)} copy(f32[16,32,512]{2,1,0:T(8,128)S(1)} %afno_block.1) | data formatting | bytes 2097152

commit v4 on v3

--- a/solution.py
+++ b/solution.py
@@ -108,8 +108,8 @@
 
 
 def kernel(
-    gain_one, spec_one, spec_two, gain_two, field, mlp_in, mlp_out, width, there, here, out,
-    f, wd, ht, hb, w1f, w2f, w1h, w1l, w2h, w2l, rw, m1h, m1l, m2h, m2l, x1h, x1l, x2h, x2l,
+    gain_one_in, spec_one_in, spec_two_in, gain_two_in, field, mlp_in, mlp_out, width, there, here, out,
+    gain_one, spec_one, spec_two, gain_two, f, wd, ht, hb, w1f, w2f, w1h, w1l, w2h, w2l, rw, m1h, m1l, m2h, m2l, x1h, x1l, x2h, x2l,
     part, parts, moments, nh, nl, fwd, got, xh, xl, zh, zl, inv, back, mixed, cells, n2, ob, ps,
     load_sem, send_sem, recv_sem,
 ):
@@ -117,11 +117,12 @@
     me_c = lax.axis_index("chan")
 
     loads = [(field.at[:, pl.ds(16 * i, 16)], f.at[:, pl.ds(16 * i, 16)]) for i in range(2)]
+    loads += [(spec_one_in, spec_one), (spec_two_in, spec_two), (gain_one_in, gain_one), (gain_two_in, gain_two)]
     loads += [(width, wd), (there, ht), (here, hb), (mlp_in, w1f), (mlp_out, w2f)]
     loads = [pltpu.make_async_copy(src, dst, load_sem.at[i]) for i, (src, dst) in enumerate(loads)]
     for load in loads[:2]:
         load.start()
-    load_width, load_there, load_here, load_in, load_out = loads[2:]
+    load_width, load_there, load_here, load_in, load_out = loads[6:]
 
     barrier = pltpu.get_barrier_semaphore()
 
@@ -181,16 +182,17 @@
             x = f[:, r : r + 8, c : c + 128]
             total = jnp.sum(x, axis=0)
             d = x - total * (1.0 / CL)
-            part[t, p, 0] = total
-            part[t, p, 1] = jnp.sum(d * d, axis=0)
+            part[p, t, 0] = total
+            part[p, t, 1] = jnp.sum(d * d, axis=0)
     for load in loads[2:]:
         load.start()
     pl.semaphore_wait(barrier, NC + NS - 2)
-    for t in range(2):
-        send_all(t, "chan", lambda p: (part.at[t, p], parts.at[t, me_c]))
-        flight[t] = part.at[t, pl.ds(0, NC - 1)]
-        parts[t, me_c] = part[t, me_c]
-
+    send_all(0, "chan", lambda p: (part.at[p], parts.at[me_c]))
+    flight[0] = part.at[pl.ds(0, NC - 1)]
+    parts[me_c] = part[me_c]
+
+    for load in loads[2:6]:
+        load.wait()
     lift = jnp.concatenate(
         [
             iota((4 * BS, BS), 0) // 2 % BS == iota((4 * BS, BS), 1),
@@ -240,17 +242,15 @@
             else:
                 x2h[b], x2l[b] = split(form[: 2 * BS])
 
-    for t in range(2):
-        arrive(parts.at[t, pl.ds(0, NC - 1)], t)
-        totals = parts[t, :, 0]
-        mean = jnp.sum(totals, axis=0) * (1.0 / C)
-        apart = totals * (1.0 / CL) - mean
-        var = (jnp.sum(parts[t, :, 1], axis=0) + CL * jnp.sum(apart * apart, axis=0)) * (1.0 / C)
-        moments[t, me_c, 0] = mean
-        moments[t, me_c, 1] = lax.rsqrt(var + 1e-05)
-
-        send_all(2 + t, "chan", lambda p: (moments.at[t, me_c], moments.at[t, me_c]))
-        flight[2 + t] = moments.at[t, pl.ds(0, NC - 1)]
+    arrive(parts.at[pl.ds(0, NC - 1)], 0)
+    totals = parts[:, :, 0]
+    mean = jnp.sum(totals, axis=0) * (1.0 / C)
+    apart = totals * (1.0 / CL) - mean
+    var = (jnp.sum(parts[:, :, 1], axis=0) + CL * jnp.sum(apart * apart, axis=0)) * (1.0 / C)
+    moments[me_c, :, 0] = mean
+    moments[me_c, :, 1] = lax.rsqrt(var + 1e-05)
+    send_all(2, "chan", lambda p: (moments.at[me_c], moments.at[me_c]))
+    flight[2] = moments.at[pl.ds(0, NC - 1)]
 
     load_in.wait()
     load_out.wait()
@@ -258,37 +258,33 @@
     w2h[...], w2l[...] = split(w2f[...])
     load_width.wait()
 
-    def send_slab(t, b):
-        channel = 4 + 2 * t + b
-        send_all(channel, "space", lambda p: (fwd.at[t, b, p], got.at[t, b, me_s]))
-        flight[channel] = fwd.at[t, b, pl.ds(0, NS - 1)]
-        got[t, b, me_s] = fwd[t, b, me_s]
-
-    for t in range(2):
-        arrive(moments.at[t, pl.ds(0, NC - 1)], 2 + t)
-        for i in range(2):
-            both = []
-            for k in (i, i + 2):
-                both.append([jnp.concatenate([moments[t, k, m], moments[t, k + 4, m]], axis=0) for m in range(2)])
-            for ch in range(CL):
-                x, x_two = (
-                    (f[ch, HH * t : HH * t + HH, c : c + 128] - mean) * scale * gain_one[ch]
-                    for c, (mean, scale) in zip((128 * i, HALF + 128 * i), both)
-                )
-                rows, lanes = slice(HH * ch, HH * ch + HH), slice(128 * i, 128 * i + 128)
-                nh[0, rows, lanes], nl[0, rows, lanes] = split(x + x_two)
-                nh[1, rows, lanes], nl[1, rows, lanes] = split(x - x_two)
+    arrive(moments.at[pl.ds(0, NC - 1)], 2)
+    for b in range(NBL):
+        for t in range(2):
+            for i in range(2):
+                both = []
+                for k in (i, i + 2):
+                    both.append([jnp.concatenate([moments[k, t, m], moments[k + 4, t, m]], axis=0) for m in range(2)])
+                for ch in range(BS):
+                    x, x_two = (
+                        (f[BS * b + ch, HH * t : HH * t + HH, c : c + 128] - mean) * scale * gain_one[BS * b + ch]
+                        for c, (mean, scale) in zip((128 * i, HALF + 128 * i), both)
+                    )
+                    row = (BS * t + ch) * HH
+                    rows, lanes = slice(row, row + HH), slice(128 * i, 128 * i + 128)
+                    nh[0, rows, lanes], nl[0, rows, lanes] = split(x + x_two)
+                    nh[1, rows, lanes], nl[1, rows, lanes] = split(x - x_two)
 
         for j in range(2):
             y = dot3((wd[0, j], wd[1, j]), (nh[j], nl[j]), NT)
-            for b in range(NBL):
-                fwd[t, b, 8 * j : 8 * j + 8] = y[:, 128 * b : 128 * b + 128].reshape(8, 2 * KC, 128)
-
-        send_slab(t, 0)
-    leave(4)
-    leave(6)
-    send_slab(0, 1)
-    send_slab(1, 1)
+            for t in range(2):
+                fwd[b, 8 * j : 8 * j + 8, t] = y[:, 128 * t : 128 * t + 128].reshape(8, 2 * KC, 128)
+
+        if b == 1:
+            leave(4)
+        send_all(4 + b, "space", lambda p: (fwd.at[b, p], got.at[b, me_s]))
+        flight[4 + b] = fwd.at[b, pl.ds(0, NS - 1)]
+        got[b, me_s] = fwd[b, me_s]
     load_there.wait()
     load_here.wait()
 
@@ -302,12 +298,10 @@
         back[b, t, me_s] = inv[b, t, me_s]
 
     def spectral(b, between=None):
+        arrive(got.at[b, pl.ds(0, NS - 1)], 4 + b)
         for t in range(2):
-            arrive(got.at[t, b, pl.ds(0, NS - 1)], 4 + 2 * t + b)
-
-        for t in range(2):
-            near = swap_eighths([got[t, b, a] for a in range(8)])
-            far = swap_eighths([got[t, b, 8 + a] for a in range(8)])
+            near = swap_eighths([got[b, a, t] for a in range(8)])
+            far = swap_eighths([got[b, 8 + a, t] for a in range(8)])
             for ch in range(BS):
                 rows, lanes = slice(2 * KC * ch, 2 * KC * ch + 2 * KC), slice(128 * t, 128 * t + 128)
                 xh[0, rows, lanes], xl[0, rows, lanes] = split(near[ch] + far[ch])
@@ -404,13 +398,13 @@
         place = out.at[:, rows, lanes]
         send_all(16 + t, "chan", lambda p: (ps.at[t, p], place))
         flight[16 + t] = ps.at[t, pl.ds(0, NC - 1)]
-        own.append(pltpu.make_async_copy(ps.at[t, me_c], place, load_sem.at[7 + t]))
+        own.append(pltpu.make_async_copy(ps.at[t, me_c], place, load_sem.at[11 + t]))
         own[t].start()
 
     spectral(0)
-    leave(8)
     send_rows(0, 1)
-    spectral(1, lambda: residual(0, 0))
+    spectral(1)
+    residual(0, 0)
     residual(0, 1)
     leave(10)
     send_rows(1, 1)
@@ -426,11 +420,12 @@
 
 
 def local(field, gain_one, spec_one, spec_two, gain_two, mlp_in, mlp_out):
-    vmem = pl.BlockSpec(memory_space=pltpu.VMEM)
-    smem = pl.BlockSpec(memory_space=pltpu.SMEM)
     hbm = pl.BlockSpec(memory_space=pl.ANY)
     tables = [jnp.asarray(table) for table in (width_table(), *height_table())]
     scratch = [
+        ((2, NBL, BS, BS), F32),
+        ((2, NBL, BS, BS), F32),
+        ((1, C), F32),
         ((CL, HL, H), F32),
         ((2, 2, HALF, HALF), BF16),
         ((2, 2, HALF, H), BF16),
@@ -450,13 +445,13 @@
         ((NBL, 4 * BS, 128), BF16),
         ((NBL, 2 * BS, 128), BF16),
         ((NBL, 2 * BS, 128), BF16),
-        ((2, NC, 2, 8, 128), F32),
-        ((2, NC, 2, 8, 128), F32),
-        ((2, NC, 2, 8, 128), F32),
+        ((NC, 2, 2, 8, 128), F32),
+        ((NC, 2, 2, 8, 128), F32),
+        ((NC, 2, 2, 8, 128), F32),
         ((2, CL * HH, HALF), BF16),
         ((2, CL * HH, HALF), BF16),
-        ((2, 2, NS, 2 * KC, 128), F32),
-        ((2, 2, NS, 2 * KC, 128), F32),
+        ((NBL, NS, 2, 2 * KC, 128), F32),
+        ((NBL, NS, 2, 2 * KC, 128), F32),
         ((2, ROWS, HALF), BF16),
         ((2, ROWS, HALF), BF16),
         ((2, ROWS, HALF), BF16),
@@ -472,10 +467,11 @@
     return pl.pallas_call(
         kernel,
         out_shape=pltpu.VMEM((CL, HL, H), F32),
-        in_specs=[smem, vmem, vmem, vmem] + [hbm] * 6,
+        in_specs=[hbm] * 10,
         out_specs=pl.BlockSpec(memory_space=pltpu.VMEM),
-        scratch_shapes=[pltpu.VMEM(shape, dtype) for shape, dtype in scratch]
-        + [pltpu.SemaphoreType.DMA((9,)), pltpu.SemaphoreType.DMA((18,)), pltpu.SemaphoreType.DMA((18,))],
+        scratch_shapes=[pltpu.SMEM((CL,), F32)]
+        + [pltpu.VMEM(shape, dtype) for shape, dtype in scratch]
+        + [pltpu.SemaphoreType.DMA((13,)), pltpu.SemaphoreType.DMA((18,)), pltpu.SemaphoreType.DMA((18,))],
         compiler_params=pltpu.CompilerParams(
             collective_id=0, has_side_effects=True, vmem_limit_bytes=56 * 1024 * 1024
         ),

time: 65.3 us -> 63.7 us (0.975)
  Pallas kernels: 64.1 us -> 62.6 us
    pallas_call x1, Pallas kernels: 64.1 us -> 62.6 us  [local(): pl.pallas_call(kernel, out_shape=pltpu.VMEM((CL, HL, H), F32), in_specs=[...]
where the time goes in v4:
time: 63.7 us; the launch traced here: 63.5 us
  Pallas kernels  62.6 us (98%)
  local copies, waits for them, and re-layouts  0.97 us (2%)
    pallas_call x1, Pallas kernels, local(): pl.pallas_call(kernel, out_shape=pltpu.VMEM((CL, HL, H), F32), in_specs=[...  62.6 us

profile of v4, /device:TPU:1, one launch (start us, length us, event | category | flops | bytes accessed | tf_op | source)
XLA Modules:
  0.0 63.5 jit_solution(16093553833082132306)
XLA Ops:
  0.0 62.6 %afno_block.1 = f32[16,32,512]{2,1,0:T(8,128)S(1)} custom-call(f32[16]{0:T(128)} %gain_one_in.1, f32[2,2,8,8]{3,2,1,0:T(8,128)} %spec_one_in.1, f32[2,2,8,8]{3,2,1,0:T(8,128)} %spec_two_in.1, f32[1,128]{1,0:T(1,128)} %bitcast.1, f32[16,32,512]{2,1,0:T(8,128)} %field.1, f32[512,128]{1,0:T(8,128)} %mlp_in.1, f32[128,512]{1,0:T(8,128)} %mlp_out.1, ...), custom_call_target="tpu_custom_call" | custom-call | tf_op jit(solution)/shard_map/afno_block/pallas_call | solution.py:467
  62.6 1.0 %copy.12 = f32[16,32,512]{2,1,0:T(8,128)} copy(f32[16,32,512]{2,1,0:T(8,128)S(1)} %afno_block.1) | data formatting | bytes 2097152

commit v5 on v4

--- a/solution.py
+++ b/solution.py
@@ -339,8 +339,6 @@
                 for n in range(2):
                     zh[n, rows], zl[n, rows] = split(z[:, HALF * n : HALF * n + HALF])
 
-        if between is not None:
-            between()
         for t in range(2):
             sums = []
             for n in range(2):
@@ -355,6 +353,8 @@
                 inv[b, t, 8 + a] = far[a]
             if t == 0:
                 send_rows(b, t)
+                if between is not None:
+                    between()
 
     def residual(b, t):
         channels = slice(BS * b, BS * b + BS)
@@ -403,8 +403,7 @@
 
     spectral(0)
     send_rows(0, 1)
-    spectral(1)
-    residual(0, 0)
+    spectral(1, lambda: residual(0, 0))
     residual(0, 1)
     leave(10)
     send_rows(1, 1)
@@ -412,11 +411,11 @@
     residual(1, 1)
     for t in range(2):
         channel_mlp(t)
+    for channel in sorted(flight):
+        leave(channel)
     for t in range(2):
         own[t].wait()
         arrive(ps.at[t, pl.ds(0, NC - 1)], 16 + t)
-    for channel in sorted(flight):
-        leave(channel)
 
 
 def local(field, gain_one, spec_one, spec_two, gain_two, mlp_in, mlp_out):

time: 63.7 us -> 63.3 us (level)
  no operation moved by 1% of the time
where the time goes in v5:
time: 63.3 us; the launch traced here: 63.1 us
  Pallas kernels  62.1 us (98%)
  local copies, waits for them, and re-layouts  0.97 us (2%)
    pallas_call x1, Pallas kernels, local(): pl.pallas_call(kernel, out_shape=pltpu.VMEM((CL, HL, H), F32), in_specs=[...  62.1 us

profile of v5, /device:TPU:1, one launch (start us, length us, event | category | flops | bytes accessed | tf_op | source)
XLA Modules:
  0.0 63.1 jit_solution(12438259223940341299)
XLA Ops:
  0.0 62.1 %afno_block.1 = f32[16,32,512]{2,1,0:T(8,128)S(1)} custom-call(f32[16]{0:T(128)} %gain_one_in.1, f32[2,2,8,8]{3,2,1,0:T(8,128)} %spec_one_in.1, f32[2,2,8,8]{3,2,1,0:T(8,128)} %spec_two_in.1, f32[1,128]{1,0:T(1,128)} %bitcast.1, f32[16,32,512]{2,1,0:T(8,128)} %field.1, f32[512,128]{1,0:T(8,128)} %mlp_in.1, f32[128,512]{1,0:T(8,128)} %mlp_out.1, ...), custom_call_target="tpu_custom_call" | custom-call | tf_op jit(solution)/shard_map/afno_block/pallas_call | solution.py:466
  62.1 1.0 %copy.12 = f32[16,32,512]{2,1,0:T(8,128)} copy(f32[16,32,512]{2,1,0:T(8,128)S(1)} %afno_block.1) | data formatting | bytes 2097152

commit v6 on v5

--- a/solution.py
+++ b/solution.py
@@ -184,12 +184,12 @@
             d = x - total * (1.0 / CL)
             part[p, t, 0] = total
             part[p, t, 1] = jnp.sum(d * d, axis=0)
-    for load in loads[2:]:
-        load.start()
     pl.semaphore_wait(barrier, NC + NS - 2)
     send_all(0, "chan", lambda p: (part.at[p], parts.at[me_c]))
     flight[0] = part.at[pl.ds(0, NC - 1)]
     parts[me_c] = part[me_c]
+    for load in loads[2:]:
+        load.start()
 
     for load in loads[2:6]:
         load.wait()

time: 63.3 us -> 63.2 us (level)
  no operation moved by 1% of the time
where the time goes in v6:
time: 63.2 us; the launch traced here: 63.1 us
  Pallas kernels  62.1 us (98%)
  local copies, waits for them, and re-layouts  0.97 us (2%)
    pallas_call x1, Pallas kernels, local(): pl.pallas_call(kernel, out_shape=pltpu.VMEM((CL, HL, H), F32), in_specs=[...  62.1 us

profile of v6, /device:TPU:1, one launch (start us, length us, event | category | flops | bytes accessed | tf_op | source)
XLA Modules:
  0.0 63.1 jit_solution(8753733329357419486)
XLA Ops:
  0.0 62.1 %afno_block.1 = f32[16,32,512]{2,1,0:T(8,128)S(1)} custom-call(f32[16]{0:T(128)} %gain_one_in.1, f32[2,2,8,8]{3,2,1,0:T(8,128)} %spec_one_in.1, f32[2,2,8,8]{3,2,1,0:T(8,128)} %spec_two_in.1, f32[1,128]{1,0:T(1,128)} %bitcast.1, f32[16,32,512]{2,1,0:T(8,128)} %field.1, f32[512,128]{1,0:T(8,128)} %mlp_in.1, f32[128,512]{1,0:T(8,128)} %mlp_out.1, ...), custom_call_target="tpu_custom_call" | custom-call | tf_op jit(solution)/shard_map/afno_block/pallas_call | solution.py:466
  62.1 1.0 %copy.12 = f32[16,32,512]{2,1,0:T(8,128)} copy(f32[16,32,512]{2,1,0:T(8,128)S(1)} %afno_block.1) | data formatting | bytes 2097152

commit v7 on v6

--- a/solution.py
+++ b/solution.py
@@ -144,6 +144,10 @@
 
     flight = {}
 
+    def far(k):
+        g = lax.rem(k + 2, 4)
+        return g + k // 2 * (1 - 2 * g)
+
     def arrive(ref, channel):
         pltpu.make_async_copy(ref, ref, recv_sem.at[channel]).wait()
 
@@ -155,10 +159,12 @@
         me, size = (me_c, NC) if axis == "chan" else (me_s, NS)
 
         def one(i, carry):
+            k = i // 2 if axis == "chan" else i // 4
+            step = far(k)
             if axis == "chan":
-                p = lax.rem(me // 2 + i // 2 + 2, 4) * 2 + lax.rem(me + i, 2)
+                p = lax.rem(me // 2 + step, 4) * 2 + lax.rem(me + i + 1, 2)
             else:
-                p = lax.rem(me // 4 + i // 4 + 2, 4) * 4 + lax.rem(me + i + 2, 4)
+                p = lax.rem(me // 4 + step, 4) * 4 + lax.rem(lax.rem(me, 4) + far(lax.rem(i, 4)), 4)
             src, dst = pair(p)
             pltpu.make_async_remote_copy(
                 src_ref=src,
@@ -170,9 +176,7 @@
             ).start()
             return carry
 
-        own = 4 if axis == "chan" else 10
-        lax.fori_loop(0, own, one, 0)
-        lax.fori_loop(own + 1, size, one, 0)
+        lax.fori_loop(0, size - 1, one, 0)
 
     for t in range(2):
         loads[t].wait()

time: 63.2 us -> 62 us (0.981)
  Pallas kernels: 62.1 us -> 60.9 us
    pallas_call x1, Pallas kernels: 62.1 us -> 60.9 us  [local(): pl.pallas_call(kernel, out_shape=pltpu.VMEM((CL, HL, H), F32), in_specs=[...]
where the time goes in v7:
time: 62 us; the launch traced here: 61.9 us
  Pallas kernels  60.9 us (98%)
  local copies, waits for them, and re-layouts  0.97 us (2%)
    pallas_call x1, Pallas kernels, local(): pl.pallas_call(kernel, out_shape=pltpu.VMEM((CL, HL, H), F32), in_specs=[...  60.9 us

profile of v7, /device:TPU:1, one launch (start us, length us, event | category | flops | bytes accessed | tf_op | source)
XLA Modules:
  0.0 61.9 jit_solution(2402350509185811535)
XLA Ops:
  0.0 60.9 %afno_block.1 = f32[16,32,512]{2,1,0:T(8,128)S(1)} custom-call(f32[16]{0:T(128)} %gain_one_in.1, f32[2,2,8,8]{3,2,1,0:T(8,128)} %spec_one_in.1, f32[2,2,8,8]{3,2,1,0:T(8,128)} %spec_two_in.1, f32[1,128]{1,0:T(1,128)} %bitcast.1, f32[16,32,512]{2,1,0:T(8,128)} %field.1, f32[512,128]{1,0:T(8,128)} %mlp_in.1, f32[128,512]{1,0:T(8,128)} %mlp_out.1, ...), custom_call_target="tpu_custom_call" | custom-call | tf_op jit(solution)/shard_map/afno_block/pallas_call | solution.py:470
  60.9 1.0 %copy.12 = f32[16,32,512]{2,1,0:T(8,128)} copy(f32[16,32,512]{2,1,0:T(8,128)S(1)} %afno_block.1) | data formatting | bytes 2097152
